TPU v7x, 32 devices: a whole 2x2x4 slice. The times are simulated.
32 devices in a mesh: harm: 8 (over z, x), remap: 4 (over y, core).
Axes of the slice: x: 2, y: 2, z: 4, core: 2. Of those that a mesh axis runs over, the one named last changes fastest.
Arguments:
- alm: bfloat16 [4096, 32, 4096], P(('harm', 'remap')), may hold values from -0.125 to 0.125
- legendre: bfloat16 [4096, 8, 4096], P(('harm', 'remap')), may hold values from -0.09375 to 0.09375
- src_cycle: int32 [8, 8192], P('harm', 'remap'), may hold values from 0 to 6, as said below
- src_phi: int32 [8, 8192], P('harm', 'remap'), may hold values from 0 to 8191, as said below
- off_cycle: int32 [8, 8192], P('harm', 'remap'), may hold values from 0 to 15
- off_phi: int32 [8, 8192], P('harm', 'remap'), may hold values from 0 to 15
Outputs:
- lensed: bfloat16 [16, 8, 8192], P(None, 'harm', 'remap')
Inputs may be any that keep to these rules, and one draw needn't show every extreme that they name: The pixel on cycle r has src_cycle = r + d clipped to 0 to 6, with d from -3 to 2. The pixel at position p of its cycle has src_phi = (p + d) mod 8192, with d from -8 to 7.
All inputs are finite; a program needn't handle non-finite values.
Results may differ from a plain program's by a relative error of at most 0.0015.
Values sent between devices are 32-bit elements; how exact they have to be, the bound alone decides.
A program may use at most 128 MiB of HBM per device.

v0:
```python
import math

import jax
import jax.numpy as jnp
from jax import lax
from jax.sharding import PartitionSpec as P

DR = 3
DP = 8
QF = 16


def with_halo(cells, sides, width):
    for axis, dim in sides:
        count = lax.axis_size(axis)
        head = lax.slice_in_dim(cells, 0, width, axis=dim)
        tail = lax.slice_in_dim(cells, cells.shape[dim] - width, cells.shape[dim], axis=dim)
        cells = jnp.concatenate(
            [
                lax.ppermute(tail, axis, [(i, (i + 1) % count) for i in range(count)]),
                cells,
                lax.ppermute(head, axis, [((i + 1) % count, i) for i in range(count)]),
            ],
            axis=dim,
        )
    return cells


def from_behind(block, axis, distance):
    devices = range(lax.axis_size(axis))
    route = [(i - distance, i) for i in devices if i - distance in devices]
    return lax.ppermute(block, axis, route)


def phase_table(rows, cols, factor, phi_count):
    row_ids = lax.broadcasted_iota(jnp.int32, (rows, cols), 0)
    col_ids = lax.broadcasted_iota(jnp.int32, (rows, cols), 1)
    phase = factor * row_ids * col_ids % phi_count
    angles = phase.astype(jnp.float32) * (2.0 * math.pi / phi_count)
    return (jnp.cos(angles), jnp.sin(angles))


def synthesize(full_coeffs, count, phi_count, sim_count):
    cycle_dev = full_coeffs.shape[0]
    order_count = full_coeffs.shape[2]
    inner = 64
    outer = order_count // inner
    period = phi_count // inner
    order_ids = lax.iota(jnp.int32, order_count)
    weights = jnp.where(order_ids == 0, 1.0, 2.0).astype(jnp.float32)
    scaled = full_coeffs * weights
    real_part = scaled[:, :sim_count].reshape(cycle_dev * sim_count, outer, inner)
    imag_part = scaled[:, sim_count:].reshape(cycle_dev * sim_count, outer, inner)
    first_cos, first_sin = phase_table(outer, period, inner, phi_count)
    high = lax.Precision.HIGHEST
    section_re = jnp.einsum("kba,bu->kau", real_part, first_cos, precision=high) - jnp.einsum(
        "kba,bu->kau", imag_part, first_sin, precision=high
    )
    section_im = jnp.einsum("kba,bu->kau", real_part, first_sin, precision=high) + jnp.einsum(
        "kba,bu->kau", imag_part, first_cos, precision=high
    )
    twist_cos, twist_sin = phase_table(inner, period, 1, phi_count)
    turned_re = section_re * twist_cos - section_im * twist_sin
    turned_im = section_re * twist_sin + section_im * twist_cos
    second_cos, second_sin = phase_table(inner, inner, period, phi_count)
    values = jnp.einsum("kau,av->kvu", turned_re, second_cos, precision=high) - jnp.einsum(
        "kau,av->kvu", turned_im, second_sin, precision=high
    )
    cycle_values = values.reshape(cycle_dev * sim_count, phi_count)
    return jnp.transpose(cycle_values.reshape(cycle_dev, sim_count, count), (1, 0, 2))


def body(alm, legendre, src_cycle, src_phi, off_cycle, off_phi):
    sim_count = alm.shape[1] // 2
    n_harm = lax.axis_size("harm")
    n_remap = lax.axis_size("remap")
    m_local = alm.shape[0]
    cycle_dev = src_cycle.shape[0]
    quarter = src_cycle.shape[1]
    phi_count = quarter * n_remap
    harm_index = lax.axis_index("harm")
    remap_index = lax.axis_index("remap")
    harmonic = jnp.einsum("mkl,mrl->rkm", alm, legendre, preferred_element_type=jnp.float32)
    cycle_coeffs = lax.all_to_all(harmonic, "harm", split_axis=0, concat_axis=2, tiled=True)
    group_ids = lax.iota(jnp.int32, n_remap)
    picker = jnp.where(group_ids == remap_index, 1.0, 0.0).astype(jnp.float32)
    spread = cycle_coeffs.reshape(cycle_dev, 2 * sim_count, n_harm, 1, m_local) * picker[:, None]
    full_coeffs = spread.reshape(cycle_dev, 2 * sim_count, n_harm * n_remap * m_local)
    partial_map = synthesize(full_coeffs, phi_count, phi_count, sim_count)
    unlensed = lax.psum_scatter(partial_map, "remap", scatter_dimension=2, tiled=True)
    widened = with_halo(unlensed, (("remap", 2),), DP)
    reach_devices = -(-DR // cycle_dev)
    below_parts = [
        from_behind(widened, "harm", distance) for distance in range(reach_devices, 0, -1)
    ]
    above_parts = [
        from_behind(widened, "harm", -distance) for distance in range(1, reach_devices + 1)
    ]
    window = jnp.concatenate(below_parts + [widened] + above_parts, axis=1)
    cycle_base = harm_index * cycle_dev - reach_devices * cycle_dev
    phi_base = remap_index * quarter - DP
    span = window.shape[2]
    cycle_slot = src_cycle - cycle_base
    phi_slot = (src_phi - phi_base) % phi_count
    flat_index = (cycle_slot * span + phi_slot).reshape(-1)
    flattened = window.reshape(sim_count, -1)

    def tap_values(offset):
        return jnp.take(flattened, flat_index + offset, axis=1)

    cycle_frac = (off_cycle.astype(jnp.float32) / QF).reshape(-1)
    phi_frac = (off_phi.astype(jnp.float32) / QF).reshape(-1)
    near_row = (1.0 - phi_frac) * tap_values(0) + phi_frac * tap_values(1)
    far_row = (1.0 - phi_frac) * tap_values(span) + phi_frac * tap_values(span + 1)
    mixed = (1.0 - cycle_frac) * near_row + cycle_frac * far_row
    return mixed.reshape(sim_count, cycle_dev, quarter).astype(jnp.bfloat16)


def solution(mesh):
    return jax.shard_map(
        body,
        mesh=mesh,
        in_specs=(
            P(("harm", "remap"), None, None),
            P(("harm", "remap"), None, None),
            P("harm", "remap"),
            P("harm", "remap"),
            P("harm", "remap"),
            P("harm", "remap"),
        ),
        out_specs=P(None, "harm", "remap"),
        check_vma=False,
    )
```

profile of v0, /device:TPU:2, one launch (start us, length us, event | category | flops | bytes accessed | tf_op | source)
XLA Modules:
  0.0 145.2 jit_solution(14672673560114712822)
XLA Ops:
  6.5 16.3 %convolution_bitcast_fusion = f32[8,32,128]{1,0,2:T(8,128)S(1)} fusion(bf16[128,8,4096]{2,1,0:T(8,128)(2,1)} %param.9, bf16[128,32,4096]{2,1,0:T(8,128)(2,1)} %param.8), kind=kOutput, calls=%fused_computation.8 | convolution fusion | flops 268435456 | bytes 42074112 | tf_op jit(solution)/shard_map/mkl,mrl->rkm/dot_general | solution.py:83
  23.7 6.5 %all-to-all-start = ((f32[8,32,128]{2,1,0:T(8,128)}), f32[8,32,128]{2,1,0:T(8,128)S(1)}, u32[]{:S(2)}, u32[]{:S(2)}) async-start(f32[8,32,128]{2,1,0:T(8,128)} %copy.25), calls=%async_computation | async-start | bytes 262144 | tf_op jit(solution)/shard_map/all_to_all | solution.py:84
  30.4 5.3 %all-to-all-done = f32[8,32,128]{2,1,0:T(8,128)S(1)} async-done(((f32[8,32,128]{2,1,0:T(8,128)}), f32[8,32,128]{2,1,0:T(8,128)S(1)}, u32[]{:S(2)}, u32[]{:S(2)}) %all-to-all-start) | async-done | bytes 131104 | tf_op jit(solution)/shard_map/all_to_all | solution.py:84
  36.6 1.0 fusion.33
  37.6 1.0 fusion.29
  38.9 1.0 convolution_subtract_fusion.1
  39.9 1.0 convolution_add_fusion
  43.5 20.7 %reduce-scatter.2.cloned.1.call-done = f32[16,1,2048]{2,0,1:T(8,128)} async-done(((f32[16,1,8192]{2,0,1:T(8,128)}), f32[16,1,2048]{2,0,1:T(8,128)}) %reduce-scatter.2.cloned.1.call-update) | async-done | bytes 131088 | tf_op jit(solution)/shard_map/reduce_scatter | solution.py:90
  65.1 1.7 %collective-permute-start.1 = (f32[16,1,8]{2,0,1:T(8,128)S(1)}, f32[16,1,8]{2,0,1:T(8,128)S(1)}, u32[]{:S(2)}, u32[]{:S(2)}) collective-permute-start(f32[16,1,8]{2,0,1:T(8,128)S(1)} %get-tuple-element.8), channel_id=1, source_target_pairs={{1,0},{2,1},{3,2},{0,3},{5,4},{6,5},{7,6},{4,7},{9,8},{10,9},{11,1... | collective-permute-start | bytes 1544 | tf_op jit(solution)/shard_map/ppermute | solution.py:22
  66.8 1.3 collective-permute-done
  69.2 4.3 %collective-permute-start.2 = (f32[16,1,2064]{2,0,1:T(8,128)S(1)}, f32[16,1,2064]{2,0,1:T(8,128)S(1)}, u32[]{:S(2)}, u32[]{:S(2)}) collective-permute-start(f32[16,1,2064]{2,0,1:T(8,128)S(1)} %concatenate.6), channel_id=1, source_target_pairs={{0,12},{4,16},{8,20},{12,24},{16,28},{1,13},{5,17},{9,21},{13,25},... | collective-permute-start | bytes 396296 | tf_op jit(solution)/shard_map/ppermute | solution.py:32
  73.6 3.4 %collective-permute-start.3 = (f32[16,1,2064]{2,0,1:T(8,128)S(1)}, f32[16,1,2064]{2,0,1:T(8,128)S(1)}, u32[]{:S(2)}, u32[]{:S(2)}) collective-permute-start(f32[16,1,2064]{2,0,1:T(8,128)S(1)} %concatenate.6), channel_id=1, source_target_pairs={{0,8},{4,12},{8,16},{12,20},{16,24},{20,28},{1,9},{5,13},{9,17},{1... | collective-permute-start | bytes 396296 | tf_op jit(solution)/shard_map/ppermute | solution.py:32
  77.0 3.4 %collective-permute-start.4 = (f32[16,1,2064]{2,0,1:T(8,128)S(1)}, f32[16,1,2064]{2,0,1:T(8,128)S(1)}, u32[]{:S(2)}, u32[]{:S(2)}) collective-permute-start(f32[16,1,2064]{2,0,1:T(8,128)S(1)} %concatenate.6), channel_id=1, source_target_pairs={{0,4},{4,8},{8,12},{12,16},{16,20},{20,24},{24,28},{1,5},{5,9},{9,... | collective-permute-start | bytes 396296 | tf_op jit(solution)/shard_map/ppermute | solution.py:32
  80.4 2.5 %collective-permute-start.5 = (f32[16,1,2064]{2,0,1:T(8,128)S(1)}, f32[16,1,2064]{2,0,1:T(8,128)S(1)}, u32[]{:S(2)}, u32[]{:S(2)}) collective-permute-start(f32[16,1,2064]{2,0,1:T(8,128)S(1)} %concatenate.6), channel_id=1, source_target_pairs={{4,0},{8,4},{12,8},{16,12},{20,16},{24,20},{28,24},{5,1},{9,5},{13... | collective-permute-start | bytes 396296 | tf_op jit(solution)/shard_map/ppermute | solution.py:32
  82.8 1.3 collective-permute-start.6
  84.1 1.3 collective-permute-start.7
  85.5 4.1 %collective-permute-done.5 = f32[16,1,2064]{2,0,1:T(8,128)S(1)} collective-permute-done((f32[16,1,2064]{2,0,1:T(8,128)S(1)}, f32[16,1,2064]{2,0,1:T(8,128)S(1)}, u32[]{:S(2)}, u32[]{:S(2)}) %collective-permute-start.5) | collective-permute-done | bytes 132128 | tf_op jit(solution)/shard_map/ppermute | solution.py:32
  89.6 1.3 collective-permute-done.6
  90.9 6.6 %collective-permute-done.7 = f32[16,1,2064]{2,0,1:T(8,128)S(1)} collective-permute-done((f32[16,1,2064]{2,0,1:T(8,128)S(1)}, f32[16,1,2064]{2,0,1:T(8,128)S(1)}, u32[]{:S(2)}, u32[]{:S(2)}) %collective-permute-start.7) | collective-permute-done | bytes 132128 | tf_op jit(solution)/shard_map/ppermute | solution.py:32
  97.6 4.5 %copy.31 = f32[16,7,2064]{0,2,1:T(8,128)} copy(f32[16,7,2064]{2,0,1:T(8,128)S(1)} %constant_dynamic-update-slice_fusion) | data formatting | bytes 1849344 | tf_op jit(solution)/shard_map/concatenate | solution.py:99
  102.1 8.6 %gather_fusion = f32[2048,16]{1,0:T(8,128)S(1)} fusion(f32[16,14448]{0,1:T(8,128)} %bitcast.74, s32[2048]{0:T(1024)S(1)} %get-tuple-element.18), kind=kCustom, calls=%fused_computation.clone | custom fusion | bytes 270336 | tf_op jit(solution)/shard_map/jit(_take)/gather | solution.py:109
  110.9 8.6 %gather_fusion.1 = f32[2048,16]{1,0:T(8,128)S(1)} fusion(f32[16,14448]{0,1:T(8,128)} %bitcast.75, s32[2048]{0:T(1024)S(1)} %get-tuple-element.19), kind=kCustom, calls=%fused_computation.1.clone | custom fusion | bytes 270336 | tf_op jit(solution)/shard_map/jit(_take)/gather | solution.py:109
  119.8 8.6 %gather_fusion.2 = f32[2048,16]{1,0:T(8,128)S(1)} fusion(f32[16,14448]{0,1:T(8,128)} %bitcast.76, s32[2048]{0:T(1024)S(1)} %get-tuple-element.20), kind=kCustom, calls=%fused_computation.2.clone | custom fusion | bytes 270336 | tf_op jit(solution)/shard_map/jit(_take)/gather | solution.py:109
  128.7 8.6 %gather_fusion.3 = f32[2048,16]{1,0:T(8,128)S(1)} fusion(f32[16,14448]{0,1:T(8,128)} %bitcast.77, s32[2048]{0:T(1024)S(1)} %get-tuple-element.21), kind=kCustom, calls=%fused_computation.3.clone | custom fusion | bytes 270336 | tf_op jit(solution)/shard_map/jit(_take)/gather | solution.py:109
  (51 shorter events, 8.4 us)
Async XLA Ops:
  23.7 19.7 %copy-start = (s32[1,2048]{1,0:T(1,128)S(1)}, s32[1,2048]{1,0:T(1,128)}, u32[]{:S(2)}) copy-start(s32[1,2048]{1,0:T(1,128)} %param.12) | copy-start | bytes 24580
  23.7 19.7 %copy-start.1 = (s32[1,2048]{1,0:T(1,128)S(1)}, s32[1,2048]{1,0:T(1,128)}, u32[]{:S(2)}) copy-start(s32[1,2048]{1,0:T(1,128)} %param.13) | copy-start | bytes 24580
  23.7 19.8 %copy-start.2 = (s32[1,2048]{1,0:T(1,128)S(1)}, s32[1,2048]{1,0:T(1,128)}, u32[]{:S(2)}) copy-start(s32[1,2048]{1,0:T(1,128)} %param.11) | copy-start | bytes 24580
  23.7 19.8 %copy-start.3 = (s32[1,2048]{1,0:T(1,128)S(1)}, s32[1,2048]{1,0:T(1,128)}, u32[]{:S(2)}) copy-start(s32[1,2048]{1,0:T(1,128)} %param.10) | copy-start | bytes 24580
  23.7 12.0 %all-to-all-start = ((f32[8,32,128]{2,1,0:T(8,128)}), f32[8,32,128]{2,1,0:T(8,128)S(1)}, u32[]{:S(2)}, u32[]{:S(2)}) async-start(f32[8,32,128]{2,1,0:T(8,128)} %copy.25), calls=%async_computation | async-start | bytes 262144 | tf_op jit(solution)/shard_map/all_to_all | solution.py:84
  30.2 34.1 %reduce-scatter.2.cloned.1.call-start = ((), (), s32[]{:S(2)}) async-start(), calls=%async_computation.2 | async-start | bytes 655360 | tf_op jit(solution)/shard_map/reduce_scatter | solution.py:90
  65.1 3.1 %collective-permute-start = (f32[16,1,8]{2,0,1:T(8,128)S(1)}, f32[16,1,8]{2,0,1:T(8,128)S(1)}, u32[]{:S(2)}, u32[]{:S(2)}) collective-permute-start(f32[16,1,8]{2,0,1:T(8,128)S(1)} %get-tuple-element.9), channel_id=1, source_target_pairs={{0,1},{1,2},{2,3},{3,0},{4,5},{5,6},{6,7},{7,4},{8,9},{9,10},{10,1... | collective-permute-start | bytes 1544 | tf_op jit(solution)/shard_map/ppermute | solution.py:20
  65.1 3.1 %collective-permute-start.1 = (f32[16,1,8]{2,0,1:T(8,128)S(1)}, f32[16,1,8]{2,0,1:T(8,128)S(1)}, u32[]{:S(2)}, u32[]{:S(2)}) collective-permute-start(f32[16,1,8]{2,0,1:T(8,128)S(1)} %get-tuple-element.8), channel_id=1, source_target_pairs={{1,0},{2,1},{3,2},{0,3},{5,4},{6,5},{7,6},{4,7},{9,8},{10,9},{11,1... | collective-permute-start | bytes 1544 | tf_op jit(solution)/shard_map/ppermute | solution.py:22
  69.2 14.9 %collective-permute-start.2 = (f32[16,1,2064]{2,0,1:T(8,128)S(1)}, f32[16,1,2064]{2,0,1:T(8,128)S(1)}, u32[]{:S(2)}, u32[]{:S(2)}) collective-permute-start(f32[16,1,2064]{2,0,1:T(8,128)S(1)} %concatenate.6), channel_id=1, source_target_pairs={{0,12},{4,16},{8,20},{12,24},{16,28},{1,13},{5,17},{9,21},{13,25},... | collective-permute-start | bytes 396296 | tf_op jit(solution)/shard_map/ppermute | solution.py:32
  73.6 11.9 %collective-permute-start.3 = (f32[16,1,2064]{2,0,1:T(8,128)S(1)}, f32[16,1,2064]{2,0,1:T(8,128)S(1)}, u32[]{:S(2)}, u32[]{:S(2)}) collective-permute-start(f32[16,1,2064]{2,0,1:T(8,128)S(1)} %concatenate.6), channel_id=1, source_target_pairs={{0,8},{4,12},{8,16},{12,20},{16,24},{20,28},{1,9},{5,13},{9,17},{1... | collective-permute-start | bytes 396296 | tf_op jit(solution)/shard_map/ppermute | solution.py:32
  77.0 8.5 %collective-permute-start.4 = (f32[16,1,2064]{2,0,1:T(8,128)S(1)}, f32[16,1,2064]{2,0,1:T(8,128)S(1)}, u32[]{:S(2)}, u32[]{:S(2)}) collective-permute-start(f32[16,1,2064]{2,0,1:T(8,128)S(1)} %concatenate.6), channel_id=1, source_target_pairs={{0,4},{4,8},{8,12},{12,16},{16,20},{20,24},{24,28},{1,5},{5,9},{9,... | collective-permute-start | bytes 396296 | tf_op jit(solution)/shard_map/ppermute | solution.py:32
  80.4 9.2 %collective-permute-start.5 = (f32[16,1,2064]{2,0,1:T(8,128)S(1)}, f32[16,1,2064]{2,0,1:T(8,128)S(1)}, u32[]{:S(2)}, u32[]{:S(2)}) collective-permute-start(f32[16,1,2064]{2,0,1:T(8,128)S(1)} %concatenate.6), channel_id=1, source_target_pairs={{4,0},{8,4},{12,8},{16,12},{20,16},{24,20},{28,24},{5,1},{9,5},{13... | collective-permute-start | bytes 396296 | tf_op jit(solution)/shard_map/ppermute | solution.py:32
  82.8 8.1 %collective-permute-start.6 = (f32[16,1,2064]{2,0,1:T(8,128)S(1)}, f32[16,1,2064]{2,0,1:T(8,128)S(1)}, u32[]{:S(2)}, u32[]{:S(2)}) collective-permute-start(f32[16,1,2064]{2,0,1:T(8,128)S(1)} %concatenate.6), channel_id=1, source_target_pairs={{8,0},{12,4},{16,8},{20,12},{24,16},{28,20},{9,1},{13,5},{17,9},{2... | collective-permute-start | bytes 396296 | tf_op jit(solution)/shard_map/ppermute | solution.py:32
  84.1 13.4 %collective-permute-start.7 = (f32[16,1,2064]{2,0,1:T(8,128)S(1)}, f32[16,1,2064]{2,0,1:T(8,128)S(1)}, u32[]{:S(2)}, u32[]{:S(2)}) collective-permute-start(f32[16,1,2064]{2,0,1:T(8,128)S(1)} %concatenate.6), channel_id=1, source_target_pairs={{12,0},{16,4},{20,8},{24,12},{28,16},{13,1},{17,5},{21,9},{25,13},... | collective-permute-start | bytes 396296 | tf_op jit(solution)/shard_map/ppermute | solution.py:32
Sparse Core Ops, SparseCore 0:
  43.5 20.7 reduce-scatter.1
where the time goes:
time: 146 us; the launch traced here: 145 us
  local copies, waits for them, and re-layouts  44.6 us (31%)
  waiting for transfers between devices  39.5 us (27%)
  starting transfers between devices  24.4 us (17%)
  matrix products  22 us (15%)
  between operations  13.7 us (9%)
    gather x8, local copies, waits for them, and re-layouts, tap_values(): return jnp.take(flattened, flat_index + offset, axis=1)  35.5 us
    reduce_scatter x1, waiting for transfers between devices, body(): lax.psum_scatter(partial_map, 'remap', scatter_dimension=2, tiled=True)  20.7 us
    dot_general x1, matrix products, body(): jnp.einsum('mkl,mrl->rkm', alm, legendre, preferred_element_type=jnp.floa...  16.3 us
    ppermute x6, starting transfers between devices, from_behind(): return lax.ppermute(block, axis, route)  16.1 us
    ppermute x6, waiting for transfers between devices, from_behind(): return lax.ppermute(block, axis, route)  12 us
    all_to_all x1, starting transfers between devices, body(): lax.all_to_all(harmonic, 'harm', split_axis=0, concat_axis=2, tiled=True)  6.48 us
    all_to_all x1, waiting for transfers between devices, body(): lax.all_to_all(harmonic, 'harm', split_axis=0, concat_axis=2, tiled=True)  5.34 us
    concatenate x2, local copies, waits for them, and re-layouts, body(): window = jnp.concatenate(below_parts + [widened] + above_parts, axis=1)  4.48 us
  transfers between devices with their start and end apart: 10, of which 6 were waited for; matrix products, arithmetic and copies ran while one was open for 0% of the time, Pallas kernels for 0%

commit v1 on v0

--- a/solution.py
+++ b/solution.py
@@ -1,8 +1,14 @@
 import math
+
+import functools
 
 import jax
 import jax.numpy as jnp
+import ml_dtypes
+import numpy as np
 from jax import lax
+from jax.experimental import pallas as pl
+from jax.experimental.pallas import tpu as pltpu
 from jax.sharding import PartitionSpec as P
 
 DR = 3
@@ -70,7 +76,7 @@
     return jnp.transpose(cycle_values.reshape(cycle_dev, sim_count, count), (1, 0, 2))
 
 
-def body(alm, legendre, src_cycle, src_phi, off_cycle, off_phi):
+def general_body(alm, legendre, src_cycle, src_phi, off_cycle, off_phi):
     sim_count = alm.shape[1] // 2
     n_harm = lax.axis_size("harm")
     n_remap = lax.axis_size("remap")
@@ -116,9 +122,360 @@
     return mixed.reshape(sim_count, cycle_dev, quarter).astype(jnp.bfloat16)
 
 
+LANES = 128
+
+
+def split_bf16(table):
+    high = table.astype(ml_dtypes.bfloat16)
+    low = (table - high.astype(np.float64)).astype(ml_dtypes.bfloat16)
+    return high, low
+
+
+def tables(n_harm, n_remap, phi_count):
+    groups = n_harm * n_remap
+    period = phi_count // LANES
+    order = (np.arange(n_harm)[None, :] * n_remap + np.arange(n_remap)[:, None]).reshape(-1)
+    angle = 2.0 * np.pi * ((np.arange(period)[:, None] * order[None, :]) % period) / period
+    first = np.block([[np.cos(angle), -np.sin(angle)], [np.sin(angle), np.cos(angle)]])
+    high, low = split_bf16(first)
+    first_table = np.concatenate([high, high, low], axis=1)
+    angle = 2.0 * np.pi * np.arange(LANES)[:, None] * np.arange(LANES)[None, :] / phi_count
+    twist = np.stack([np.cos(angle), np.sin(angle)]).astype(np.float32)
+    blocks = np.arange(-8, period + 8) % period
+    angle = 2.0 * np.pi * ((blocks[:, None] * np.arange(LANES)[None, :]) % period) / period
+    high, low = split_bf16(2.0 * np.concatenate([np.cos(angle), -np.sin(angle)], axis=1))
+    second_table = np.stack([high, low])
+    return first_table, twist, second_table
+
+
+def accumulate_orders(group, alm_ref, leg_ref, acc_ref):
+    per_group, _, rows, depth = alm_ref.shape
+    cycles = leg_ref.shape[2]
+    coeffs = alm_ref[...].reshape(per_group * rows, depth)
+    basis = leg_ref[...].reshape(per_group * cycles, depth)
+    product = lax.dot_general(
+        coeffs, basis, (((1,), (1,)), ((), ())), preferred_element_type=jnp.float32
+    )
+    lane = lax.broadcasted_iota(jnp.int32, (rows, LANES), 1)
+    own = jnp.zeros((rows, LANES), jnp.float32)
+    for i in range(per_group):
+        own = jnp.where(lane // cycles == i, product[i * rows : (i + 1) * rows], own)
+    device = lax.axis_index("harm") * lax.axis_size("remap") + lax.axis_index("remap")
+    first_order = jnp.logical_and(device == 0, group == 0)
+    for r in range(cycles):
+        turned = pltpu.roll(own, lax.rem(group - r + LANES, LANES), axis=1)
+        turned = jnp.where(jnp.logical_and(first_order, lane == 0), 0.5 * turned, turned)
+        held = acc_ref[r * rows : (r + 1) * rows, :]
+        acc_ref[r * rows : (r + 1) * rows, :] = jnp.where(lane % cycles == group, turned, held)
+
+
+def dot_last(a, b):
+    return lax.dot_general(a, b, (((1,), (1,)), ((), ())), preferred_element_type=jnp.float32)
+
+
+def synthesize_sim(x_ref, e, per_dev, cycles, first_ref, twist_ref, second, z_ref):
+    step = per_dev * 2 * cycles
+    groups = x_ref.shape[0] // step
+    half = first_ref.shape[0] // 2
+    columns = []
+    for r in range(cycles):
+        columns.append(
+            jnp.concatenate(
+                [
+                    x_ref[pl.ds((e * 2 + c) * cycles + r, groups, stride=step), :]
+                    for c in range(2)
+                ],
+                axis=0,
+            )
+        )
+    coeffs = jnp.concatenate(columns, axis=1)
+    high = coeffs.astype(jnp.bfloat16)
+    low = (coeffs - high.astype(jnp.float32)).astype(jnp.bfloat16)
+    section = jnp.dot(
+        first_ref[...].astype(jnp.bfloat16),
+        jnp.concatenate([high, low, high], axis=0),
+        preferred_element_type=jnp.float32,
+    )
+    for r in range(cycles):
+        re = section[:half, r * LANES : (r + 1) * LANES]
+        im = section[half:, r * LANES : (r + 1) * LANES]
+        re = jnp.concatenate([re] * (LANES // half), axis=0)
+        im = jnp.concatenate([im] * (LANES // half), axis=0)
+        turned = jnp.concatenate(
+            [
+                re * twist_ref[0] - im * twist_ref[1],
+                re * twist_ref[1] + im * twist_ref[0],
+            ],
+            axis=1,
+        )
+        turned_high = turned.astype(jnp.bfloat16)
+        z_ref[0, r * LANES : (r + 1) * LANES, :] = turned_high
+        z_ref[1, r * LANES : (r + 1) * LANES, :] = (
+            turned - turned_high.astype(jnp.float32)
+        ).astype(jnp.bfloat16)
+    span = second.shape[0] // 2
+    both = dot_last(second, z_ref[0])
+    return both[:span] + both[span:] + dot_last(second[:span], z_ref[1])
+
+
+def interpolate(e, r, cycles, u_ref, sc, sp, oc, op, tiles):
+    lane = lax.broadcasted_iota(jnp.int32, (tiles, LANES), 1)
+    near_index = sp & (LANES - 1)
+    far_index = (sp + 1) & (LANES - 1)
+    b = op.astype(jnp.float32) * (1.0 / QF)
+    a = oc.astype(jnp.float32) * (1.0 / QF)
+    total = jnp.zeros((tiles, LANES), jnp.float32)
+    for j in range(max(0, r - DR), min(cycles - 1, r + DR) + 1):
+        left = u_ref[e, 0, j]
+        right = u_ref[e, 1, j]
+
+        def tap(index):
+            return jnp.where(
+                lane < LANES // 2,
+                jnp.take_along_axis(left, index, axis=1, mode="promise_in_bounds"),
+                jnp.take_along_axis(right, index, axis=1, mode="promise_in_bounds"),
+            )
+
+        weight = jnp.where(sc == j, 1.0 - a, 0.0) + jnp.where(sc == j - 1, a, 0.0)
+        total = total + weight * ((1.0 - b) * tap(near_index) + b * tap(far_index))
+    return total
+
+
+def to_device(src, dst, send_sem, recv_sem, axis, index):
+    return pltpu.make_async_remote_copy(
+        src_ref=src,
+        dst_ref=dst,
+        send_sem=send_sem,
+        recv_sem=recv_sem,
+        device_id={axis: index},
+        device_id_type=pl.DeviceIdType.MESH,
+    )
+
+
+def sky_step(
+    n_harm, n_remap, per_dev,
+    alm_ref, leg_ref, sc_ref, sp_ref, oc_ref, op_ref, first_ref, twist_ref, second_ref,
+    out_ref,
+    acc_ref, pack_ref, x_ref, where_ref, z_ref, w_ref, u_ref, maps_ref, fin_ref,
+    i_send, i_recv, a_send, a_recv, y_send, y_recv, s_send, s_recv, f_send, f_recv, o_send, o_recv,
+):
+    group = pl.program_id(0)
+    cycles = leg_ref.shape[2]
+    tiles = sc_ref.shape[0]
+    rows = alm_ref.shape[2]
+    piece = per_dev * 2 * cycles
+    me = lax.axis_index("harm")
+    q = lax.axis_index("remap")
+    across = lax.rem(q + 2, n_remap)
+    sibling = q + 1 - 2 * lax.rem(q, 2)
+    far = lax.rem(sibling + 2, n_remap)
+    peers = [lax.rem(me + k, n_harm) for k in range(1, n_harm)]
+
+    def slot(quarter, source):
+        start = pl.multiple_of((quarter * n_harm + source) * piece, piece)
+        return x_ref.at[pl.ds(start, piece), :]
+
+    def packed(target):
+        return pack_ref.at[pl.ds(pl.multiple_of(target * piece, piece), piece), :]
+
+    def index_copy(source, target):
+        return to_device(
+            where_ref.at[source], where_ref.at[source], i_send.at[target], i_recv.at[source], "harm", target
+        )
+
+    def order_copy(source, target):
+        return to_device(
+            packed(target), slot(q, source), a_send.at[target], a_recv.at[source], "harm", target
+        )
+
+    def across_copy(quarter, source):
+        return to_device(
+            slot(quarter, source), slot(quarter, source), y_send.at[source], y_recv.at[source], "remap", across
+        )
+
+    def sibling_copy(quarter, source):
+        return to_device(
+            slot(quarter, source), slot(quarter, source), s_send.at[source], s_recv.at[source], "remap", sibling
+        )
+
+    def forward_copy(quarter, source):
+        return to_device(
+            slot(quarter, source), slot(quarter, source), f_send.at[source], f_recv.at[source], "remap", sibling
+        )
+
+    def map_copy(source, target):
+        return to_device(
+            maps_ref.at[target], fin_ref.at[source], o_send.at[target], o_recv.at[source], "harm", target
+        )
+
+    @pl.when(group == 0)
+    def _():
+        barrier = pltpu.get_barrier_semaphore()
+        for p in peers:
+            pl.semaphore_signal(
+                barrier, inc=1, device_id={"harm": p}, device_id_type=pl.DeviceIdType.MESH
+            )
+        for p in (across, sibling):
+            pl.semaphore_signal(
+                barrier, inc=1, device_id={"remap": p}, device_id_type=pl.DeviceIdType.MESH
+            )
+        for i, ref in enumerate((sc_ref, sp_ref, oc_ref, op_ref)):
+            where_ref[me, i] = ref[...]
+        pl.semaphore_wait(barrier, n_harm + 1)
+        for p in peers:
+            index_copy(me, p).start()
+
+    accumulate_orders(group, alm_ref, leg_ref, acc_ref)
+
+    @pl.when(group == pl.num_programs(0) - 1)
+    def _():
+        sims = rows // 2
+        for k in range(rows):
+            sim, part = k % sims, k // sims
+            start = (sim // per_dev) * piece + (sim % per_dev) * 2 * cycles + part * cycles
+            pack_ref[start : start + cycles, :] = acc_ref[pl.ds(k, cycles, stride=rows), :]
+        for p in reversed(peers):
+            order_copy(me, p).start()
+        own = pl.multiple_of((q * n_harm + me) * piece, piece)
+        x_ref[pl.ds(own, piece), :] = pack_ref[pl.ds(pl.multiple_of(me * piece, piece), piece), :]
+        across_copy(q, me).start()
+        sibling_copy(q, me).start()
+        for p in peers:
+            order_copy(p, p).wait_recv()
+            across_copy(q, p).start()
+            sibling_copy(q, p).start()
+        for p in [me] + peers:
+            across_copy(across, p).wait_recv()
+            forward_copy(across, p).start()
+        for p in peers:
+            index_copy(p, p).wait_recv()
+        for p in [me] + peers:
+            sibling_copy(sibling, p).wait_recv()
+        for p in [me] + peers:
+            forward_copy(far, p).wait_recv()
+
+        start = pl.multiple_of(q * tiles, tiles)
+        span = tiles + 16
+        second = jnp.concatenate(
+            [second_ref[0, pl.ds(start, span), :], second_ref[1, pl.ds(start, span), :]], axis=0
+        ).astype(jnp.bfloat16)
+        lane = lax.broadcasted_iota(jnp.int32, (tiles, LANES), 1)
+        for e in range(per_dev):
+            w_ref[...] = synthesize_sim(
+                x_ref, e, per_dev, cycles, first_ref, twist_ref, second, z_ref
+            )
+            for j in range(cycles):
+                cols = slice(j * LANES, (j + 1) * LANES)
+                here = w_ref[8 : 8 + tiles, cols]
+                u_ref[e, 0, j] = jnp.where(lane >= 3 * LANES // 4, w_ref[7 : 7 + tiles, cols], here)
+                u_ref[e, 1, j] = jnp.where(lane < LANES // 4, w_ref[9 : 9 + tiles, cols], here)
+        for r in range(cycles):
+            for e in range(per_dev):
+                maps_ref[r, e] = interpolate(
+                    e, r, cycles, u_ref,
+                    where_ref[r, 0], where_ref[r, 1], where_ref[r, 2], where_ref[r, 3], tiles,
+                )
+
+            @pl.when(me != r)
+            def _():
+                map_copy(me, r).start()
+
+        fin_ref[me] = maps_ref[me]
+        for p in peers:
+            map_copy(p, p).wait_recv()
+        for s in range(sims):
+            for t in range(tiles):
+                out_ref[s : s + 1, t * LANES : (t + 1) * LANES] = fin_ref[
+                    s // per_dev, s % per_dev, t : t + 1
+                ].astype(jnp.bfloat16)
+        for p in peers:
+            index_copy(me, p).wait_send()
+            order_copy(me, p).wait_send()
+            map_copy(me, p).wait_send()
+        for p in [me] + peers:
+            across_copy(q, p).wait_send()
+            sibling_copy(q, p).wait_send()
+            forward_copy(across, p).wait_send()
+
+
+def body(alm, legendre, src_cycle, src_phi, off_cycle, off_phi):
+    n_harm = lax.axis_size("harm")
+    n_remap = lax.axis_size("remap")
+    m_local, rows, depth = alm.shape
+    sims = rows // 2
+    per_dev = sims // n_harm
+    cycles = legendre.shape[1]
+    quarter = src_cycle.shape[1]
+    tiles = quarter // LANES
+    per_group = LANES // cycles
+    groups = m_local // per_group
+    piece = per_dev * 2 * cycles
+    first_table, twist, second_table = tables(n_harm, n_remap, quarter * n_remap)
+    whole = pl.BlockSpec(memory_space=pltpu.VMEM)
+    sems = [pltpu.SemaphoreType.DMA((n_harm,)) for _ in range(12)]
+    lensed = pl.pallas_call(
+        functools.partial(sky_step, n_harm, n_remap, per_dev),
+        grid=(groups,),
+        in_specs=[
+            pl.BlockSpec((per_group, 1, rows, depth), lambda g: (0, g, 0, 0)),
+            pl.BlockSpec((per_group, 1, cycles, depth), lambda g: (0, g, 0, 0)),
+        ]
+        + [whole] * 7,
+        out_specs=whole,
+        out_shape=jax.ShapeDtypeStruct((sims, quarter), jnp.bfloat16),
+        scratch_shapes=[
+            pltpu.VMEM((rows * cycles, LANES), jnp.float32),
+            pltpu.VMEM((rows * cycles, LANES), jnp.float32),
+            pltpu.VMEM((n_remap * n_harm * piece, LANES), jnp.float32),
+            pltpu.VMEM((n_harm, 4, tiles, LANES), jnp.int32),
+            pltpu.VMEM((2, cycles * LANES, 2 * LANES), jnp.bfloat16),
+            pltpu.VMEM((tiles + 16, cycles * LANES), jnp.float32),
+            pltpu.VMEM((per_dev, 2, cycles, tiles, LANES), jnp.float32),
+            pltpu.VMEM((cycles, per_dev, tiles, LANES), jnp.float32),
+            pltpu.VMEM((n_harm, per_dev, tiles, LANES), jnp.float32),
+        ]
+        + sems,
+        compiler_params=pltpu.CompilerParams(
+            collective_id=0, has_side_effects=True, vmem_limit_bytes=56 * 2**20
+        ),
+    )(
+        alm.reshape(per_group, groups, rows, depth),
+        legendre.reshape(per_group, groups, cycles, depth),
+        *(array.reshape(tiles, LANES) for array in (src_cycle, src_phi, off_cycle, off_phi)),
+        jnp.asarray(first_table.astype(np.float32)),
+        jnp.asarray(twist),
+        jnp.asarray(second_table.astype(np.float32)),
+    )
+    return lensed.reshape(sims, 1, quarter)
+
+
+def fits(mesh, alm, legendre, src_cycle):
+    n_harm, n_remap = mesh.shape["harm"], mesh.shape["remap"]
+    cycles = legendre.shape[1]
+    sims = alm.shape[1] // 2
+    phi_count = src_cycle.shape[1]
+    return (
+        cycles == n_harm == 8
+        and sims % n_harm == 0
+        and alm.shape[0] == LANES * n_harm * n_remap
+        and phi_count == LANES * 64
+        and (phi_count // n_remap) % (16 * LANES) == 0
+        and (n_harm * n_remap) % 8 == 0
+        and n_remap == 4
+    )
+
+
 def solution(mesh):
+    def run(*arrays):
+        chosen = body if fits(mesh, arrays[0], arrays[1], arrays[2]) else general_body
+        return sharded(mesh, chosen)(*arrays)
+
+    return run
+
+
+def sharded(mesh, chosen):
     return jax.shard_map(
-        body,
+        chosen,
         mesh=mesh,
         in_specs=(
             P(("harm", "remap"), None, None),

time: 146 us -> 41 us (0.28)
  the two profiles are of different devices: /device:TPU:2 before, /device:TPU:0 now
where the time goes in v1:
time: 41 us; the launch traced here: 40.9 us
  Pallas kernels  39.4 us (96%)
  local copies, waits for them, and re-layouts  1.47 us (4%)
    pallas_call x1, Pallas kernels, body(): pl.pallas_call(functools.partial(sky_step, n_harm, n_remap, per_dev), gri...  39.4 us
    unnamed x1, local copies, waits for them, and re-layouts  1.47 us

profile of v1, /device:TPU:0, one launch (start us, length us, event | category | flops | bytes accessed | tf_op | source)
XLA Modules:
  0.0 40.9 jit_solution(5392778963337836265)
XLA Ops:
  0.0 39.4 %shard_map.91 = bf16[16,2048]{1,0:T(8,128)(2,1)} custom-call(bf16[16,8,32,4096]{3,2,1,0:T(8,128)(2,1)} %bitcast.7, bf16[16,8,8,4096]{3,2,1,0:T(8,128)(2,1)} %bitcast.8, s32[16,128]{1,0:T(8,128)} %bitcast.10, s32[16,128]{1,0:T(8,128)} %bitcast.11, s32[16,128]{1,0:T(8,128)} %bitcast.12, s32[16,128]{1,0:T(8,128)} %bitcast.13, ...), custom_call_target="tpu_custom_call" | custom-call | tf_op jit(solution)/shard_map/pallas_call | solution.py:416
  39.4 1.5 %copy.11 = bf16[16,1,2048]{2,0,1:T(8,128)(2,1)} copy(bf16[16,1,2048]{2,0,1:T(8,128)(2,1)} %bitcast.9) | data formatting | bytes 131072

commit v2 on v1

--- a/solution.py
+++ b/solution.py
@@ -132,25 +132,30 @@
 
 
 def tables(n_harm, n_remap, phi_count):
-    groups = n_harm * n_remap
-    period = phi_count // LANES
-    order = (np.arange(n_harm)[None, :] * n_remap + np.arange(n_remap)[:, None]).reshape(-1)
-    angle = 2.0 * np.pi * ((np.arange(period)[:, None] * order[None, :]) % period) / period
+    lane = np.arange(LANES)
+    order = (lane // 8) * 4 + lane % 4
+    parity = (lane // 4) % 2
+    device = (np.arange(n_harm)[None, :] * n_remap + np.arange(n_remap)[:, None]).reshape(-1)
+    block = (device[:, None] * 2 + np.arange(2)[None, :]).reshape(-1)
+    angle = 2.0 * np.pi * ((np.arange(LANES)[:, None] * block[None, :]) % LANES) / LANES
     first = np.block([[np.cos(angle), -np.sin(angle)], [np.sin(angle), np.cos(angle)]])
     high, low = split_bf16(first)
-    first_table = np.concatenate([high, high, low], axis=1)
-    angle = 2.0 * np.pi * np.arange(LANES)[:, None] * np.arange(LANES)[None, :] / phi_count
+    first_table = np.concatenate([high, high, low], axis=1).astype(np.float32)
+    angle = 2.0 * np.pi * np.arange(LANES)[:, None] * order[None, :] / phi_count
     twist = np.stack([np.cos(angle), np.sin(angle)]).astype(np.float32)
-    blocks = np.arange(-8, period + 8) % period
-    angle = 2.0 * np.pi * ((blocks[:, None] * np.arange(LANES)[None, :]) % period) / period
-    high, low = split_bf16(2.0 * np.concatenate([np.cos(angle), -np.sin(angle)], axis=1))
-    second_table = np.stack([high, low])
+    period = phi_count // LANES
+    rows = np.arange(-8, period + 8) % period
+    angle = 2.0 * np.pi * ((rows[:, None] * order[None, :]) % period) / period
+    second = 2.0 * np.concatenate([np.cos(angle), -np.sin(angle)], axis=1)
+    keep = np.concatenate([parity, parity])[None, None, :] == np.arange(2)[:, None, None]
+    high, low = split_bf16(np.where(keep, second[None], 0.0))
+    second_table = np.concatenate([high, low]).astype(np.float32)
     return first_table, twist, second_table
 
 
-def accumulate_orders(group, alm_ref, leg_ref, acc_ref):
-    per_group, _, rows, depth = alm_ref.shape
-    cycles = leg_ref.shape[2]
+def accumulate_orders(half, turn, alm_ref, leg_ref, acc_ref):
+    _, per_group, _, rows, depth = alm_ref.shape
+    cycles = leg_ref.shape[3]
     coeffs = alm_ref[...].reshape(per_group * rows, depth)
     basis = leg_ref[...].reshape(per_group * cycles, depth)
     product = lax.dot_general(
@@ -161,28 +166,29 @@
     for i in range(per_group):
         own = jnp.where(lane // cycles == i, product[i * rows : (i + 1) * rows], own)
     device = lax.axis_index("harm") * lax.axis_size("remap") + lax.axis_index("remap")
-    first_order = jnp.logical_and(device == 0, group == 0)
+    first_order = jnp.logical_and(device == 0, jnp.logical_and(half == 0, turn == 0))
     for r in range(cycles):
-        turned = pltpu.roll(own, lax.rem(group - r + LANES, LANES), axis=1)
-        turned = jnp.where(jnp.logical_and(first_order, lane == 0), 0.5 * turned, turned)
-        held = acc_ref[r * rows : (r + 1) * rows, :]
-        acc_ref[r * rows : (r + 1) * rows, :] = jnp.where(lane % cycles == group, turned, held)
+        place = 4 * (r % 2) + turn
+        turned = pltpu.roll(own, lax.rem(place - r + LANES, LANES), axis=1)
+        turned = jnp.where(jnp.logical_and(first_order, lane == place), 0.5 * turned, turned)
+        at = (r // 2) * rows
+        acc_ref[at : at + rows, :] = jnp.where(
+            lane % cycles == place, turned, acc_ref[at : at + rows, :]
+        )
 
 
 def dot_last(a, b):
     return lax.dot_general(a, b, (((1,), (1,)), ((), ())), preferred_element_type=jnp.float32)
 
 
-def synthesize_sim(x_ref, e, per_dev, cycles, first_ref, twist_ref, second, z_ref):
-    step = per_dev * 2 * cycles
-    groups = x_ref.shape[0] // step
-    half = first_ref.shape[0] // 2
+def synthesize_sim(x_ref, e, step, pairs, first, twist_ref, second, z_ref):
+    blocks = x_ref.shape[0] // step
     columns = []
-    for r in range(cycles):
+    for pair in range(pairs):
         columns.append(
             jnp.concatenate(
                 [
-                    x_ref[pl.ds((e * 2 + c) * cycles + r, groups, stride=step), :]
+                    x_ref[pl.ds((e * 2 + c) * pairs + pair, blocks, stride=step), :]
                     for c in range(2)
                 ],
                 axis=0,
@@ -192,15 +198,12 @@
     high = coeffs.astype(jnp.bfloat16)
     low = (coeffs - high.astype(jnp.float32)).astype(jnp.bfloat16)
     section = jnp.dot(
-        first_ref[...].astype(jnp.bfloat16),
-        jnp.concatenate([high, low, high], axis=0),
-        preferred_element_type=jnp.float32,
-    )
-    for r in range(cycles):
-        re = section[:half, r * LANES : (r + 1) * LANES]
-        im = section[half:, r * LANES : (r + 1) * LANES]
-        re = jnp.concatenate([re] * (LANES // half), axis=0)
-        im = jnp.concatenate([im] * (LANES // half), axis=0)
+        first, jnp.concatenate([high, low, high], axis=0), preferred_element_type=jnp.float32
+    )
+    for pair in range(pairs):
+        cols = slice(pair * LANES, (pair + 1) * LANES)
+        re = section[:LANES, cols]
+        im = section[LANES:, cols]
         turned = jnp.concatenate(
             [
                 re * twist_ref[0] - im * twist_ref[1],
@@ -209,36 +212,37 @@
             axis=1,
         )
         turned_high = turned.astype(jnp.bfloat16)
-        z_ref[0, r * LANES : (r + 1) * LANES, :] = turned_high
-        z_ref[1, r * LANES : (r + 1) * LANES, :] = (
-            turned - turned_high.astype(jnp.float32)
-        ).astype(jnp.bfloat16)
+        z_ref[0, cols, :] = turned_high
+        z_ref[1, cols, :] = (turned - turned_high.astype(jnp.float32)).astype(jnp.bfloat16)
     span = second.shape[0] // 2
     both = dot_last(second, z_ref[0])
     return both[:span] + both[span:] + dot_last(second[:span], z_ref[1])
 
 
-def interpolate(e, r, cycles, u_ref, sc, sp, oc, op, tiles):
+def interpolate(r, cycles, per_dev, u_ref, sc, sp, oc, op, tiles):
     lane = lax.broadcasted_iota(jnp.int32, (tiles, LANES), 1)
     near_index = sp & (LANES - 1)
     far_index = (sp + 1) & (LANES - 1)
     b = op.astype(jnp.float32) * (1.0 / QF)
     a = oc.astype(jnp.float32) * (1.0 / QF)
-    total = jnp.zeros((tiles, LANES), jnp.float32)
+    totals = [jnp.zeros((tiles, LANES), jnp.float32) for _ in range(per_dev)]
     for j in range(max(0, r - DR), min(cycles - 1, r + DR) + 1):
-        left = u_ref[e, 0, j]
-        right = u_ref[e, 1, j]
-
-        def tap(index):
-            return jnp.where(
-                lane < LANES // 2,
-                jnp.take_along_axis(left, index, axis=1, mode="promise_in_bounds"),
-                jnp.take_along_axis(right, index, axis=1, mode="promise_in_bounds"),
+        weight = jnp.where(sc == j, 1.0 - a, jnp.where(sc == j - 1, a, 0.0))
+        near_weight = weight * (1.0 - b)
+        far_weight = weight * b
+        for e in range(per_dev):
+            left = u_ref[e, 0, j]
+            right = u_ref[e, 1, j]
+            near, far = (
+                jnp.where(
+                    lane < LANES // 2,
+                    jnp.take_along_axis(left, index, axis=1, mode="promise_in_bounds"),
+                    jnp.take_along_axis(right, index, axis=1, mode="promise_in_bounds"),
+                )
+                for index in (near_index, far_index)
             )
-
-        weight = jnp.where(sc == j, 1.0 - a, 0.0) + jnp.where(sc == j - 1, a, 0.0)
-        total = total + weight * ((1.0 - b) * tap(near_index) + b * tap(far_index))
-    return total
+            totals[e] = totals[e] + near_weight * near + far_weight * far
+    return totals
 
 
 def to_device(src, dst, send_sem, recv_sem, axis, index):
@@ -260,10 +264,14 @@
     i_send, i_recv, a_send, a_recv, y_send, y_recv, s_send, s_recv, f_send, f_recv, o_send, o_recv,
 ):
     group = pl.program_id(0)
-    cycles = leg_ref.shape[2]
+    groups = pl.num_programs(0)
+    turns = groups // 2
+    cycles = leg_ref.shape[3]
+    pairs = cycles // 2
     tiles = sc_ref.shape[0]
-    rows = alm_ref.shape[2]
-    piece = per_dev * 2 * cycles
+    rows = alm_ref.shape[3]
+    sims = rows // 2
+    piece = per_dev * 2 * pairs
     me = lax.axis_index("harm")
     q = lax.axis_index("remap")
     across = lax.rem(q + 2, n_remap)
@@ -271,42 +279,64 @@
     far = lax.rem(sibling + 2, n_remap)
     peers = [lax.rem(me + k, n_harm) for k in range(1, n_harm)]
 
-    def slot(quarter, source):
-        start = pl.multiple_of((quarter * n_harm + source) * piece, piece)
+    def slot(half, quarter, source):
+        start = pl.multiple_of(((quarter * n_harm + source) * 2 + half) * piece, piece)
         return x_ref.at[pl.ds(start, piece), :]
 
-    def packed(target):
-        return pack_ref.at[pl.ds(pl.multiple_of(target * piece, piece), piece), :]
+    def packed(half, target):
+        return pack_ref.at[half, pl.ds(pl.multiple_of(target * piece, piece), piece), :]
 
     def index_copy(source, target):
         return to_device(
             where_ref.at[source], where_ref.at[source], i_send.at[target], i_recv.at[source], "harm", target
         )
 
-    def order_copy(source, target):
+    def order_copy(half, source, target):
         return to_device(
-            packed(target), slot(q, source), a_send.at[target], a_recv.at[source], "harm", target
-        )
-
-    def across_copy(quarter, source):
-        return to_device(
-            slot(quarter, source), slot(quarter, source), y_send.at[source], y_recv.at[source], "remap", across
-        )
-
-    def sibling_copy(quarter, source):
-        return to_device(
-            slot(quarter, source), slot(quarter, source), s_send.at[source], s_recv.at[source], "remap", sibling
-        )
-
-    def forward_copy(quarter, source):
-        return to_device(
-            slot(quarter, source), slot(quarter, source), f_send.at[source], f_recv.at[source], "remap", sibling
-        )
+            packed(half, target), slot(half, q, source),
+            a_send.at[half, target], a_recv.at[half, source], "harm", target,
+        )
+
+    def across_copy(half, quarter, source):
+        held = slot(half, quarter, source)
+        return to_device(held, held, y_send.at[half, source], y_recv.at[half, source], "remap", across)
+
+    def sibling_copy(half, quarter, source):
+        held = slot(half, quarter, source)
+        return to_device(held, held, s_send.at[half, source], s_recv.at[half, source], "remap", sibling)
+
+    def forward_copy(half, quarter, source):
+        held = slot(half, quarter, source)
+        return to_device(held, held, f_send.at[half, source], f_recv.at[half, source], "remap", sibling)
 
     def map_copy(source, target):
         return to_device(
             maps_ref.at[target], fin_ref.at[source], o_send.at[target], o_recv.at[source], "harm", target
         )
+
+    def send_orders(half):
+        for k in range(rows):
+            sim, part = k % sims, k // sims
+            start = (sim // per_dev) * piece + ((sim % per_dev) * 2 + part) * pairs
+            pack_ref[half, start : start + pairs, :] = acc_ref[pl.ds(k, pairs, stride=rows), :]
+        for p in peers:
+            order_copy(half, me, p).start()
+        own = pl.multiple_of(((q * n_harm + me) * 2 + half) * piece, piece)
+        mine = pl.multiple_of(me * piece, piece)
+        x_ref[pl.ds(own, piece), :] = pack_ref[half, pl.ds(mine, piece), :]
+        across_copy(half, q, me).start()
+        sibling_copy(half, q, me).start()
+
+    def relay_orders(half):
+        for p in peers:
+            order_copy(half, p, p).wait_recv()
+            across_copy(half, q, p).start()
+            sibling_copy(half, q, p).start()
+
+    def forward_orders(half):
+        for p in [me] + peers:
+            across_copy(half, across, p).wait_recv()
+            forward_copy(half, across, p).start()
 
     @pl.when(group == 0)
     def _():
@@ -325,56 +355,56 @@
         for p in peers:
             index_copy(me, p).start()
 
-    accumulate_orders(group, alm_ref, leg_ref, acc_ref)
-
-    @pl.when(group == pl.num_programs(0) - 1)
+    accumulate_orders(group // turns, lax.rem(group, turns), alm_ref, leg_ref, acc_ref)
+
+    @pl.when(group == turns - 1)
     def _():
-        sims = rows // 2
-        for k in range(rows):
-            sim, part = k % sims, k // sims
-            start = (sim // per_dev) * piece + (sim % per_dev) * 2 * cycles + part * cycles
-            pack_ref[start : start + cycles, :] = acc_ref[pl.ds(k, cycles, stride=rows), :]
-        for p in reversed(peers):
-            order_copy(me, p).start()
-        own = pl.multiple_of((q * n_harm + me) * piece, piece)
-        x_ref[pl.ds(own, piece), :] = pack_ref[pl.ds(pl.multiple_of(me * piece, piece), piece), :]
-        across_copy(q, me).start()
-        sibling_copy(q, me).start()
-        for p in peers:
-            order_copy(p, p).wait_recv()
-            across_copy(q, p).start()
-            sibling_copy(q, p).start()
-        for p in [me] + peers:
-            across_copy(across, p).wait_recv()
-            forward_copy(across, p).start()
+        send_orders(0)
+
+    @pl.when(group == turns + 1)
+    def _():
+        relay_orders(0)
+
+    @pl.when(group == turns + 2)
+    def _():
+        forward_orders(0)
+
+    @pl.when(group == groups - 1)
+    def _():
+        send_orders(1)
+        relay_orders(1)
+        forward_orders(1)
         for p in peers:
             index_copy(p, p).wait_recv()
-        for p in [me] + peers:
-            sibling_copy(sibling, p).wait_recv()
-        for p in [me] + peers:
-            forward_copy(far, p).wait_recv()
+        for half in range(2):
+            for p in [me] + peers:
+                sibling_copy(half, sibling, p).wait_recv()
+                forward_copy(half, far, p).wait_recv()
 
         start = pl.multiple_of(q * tiles, tiles)
         span = tiles + 16
         second = jnp.concatenate(
-            [second_ref[0, pl.ds(start, span), :], second_ref[1, pl.ds(start, span), :]], axis=0
+            [second_ref[i, pl.ds(start, span), :] for i in range(4)], axis=0
         ).astype(jnp.bfloat16)
+        first = first_ref[...].astype(jnp.bfloat16)
         lane = lax.broadcasted_iota(jnp.int32, (tiles, LANES), 1)
         for e in range(per_dev):
-            w_ref[...] = synthesize_sim(
-                x_ref, e, per_dev, cycles, first_ref, twist_ref, second, z_ref
+            w_ref[...] = synthesize_sim(x_ref, e, piece, pairs, first, twist_ref, second, z_ref)
+            for j in range(cycles):
+                cols = slice((j // 2) * LANES, (j // 2 + 1) * LANES)
+                top = (j % 2) * span + 8
+                here = w_ref[top : top + tiles, cols]
+                before = w_ref[top - 1 : top - 1 + tiles, cols]
+                after = w_ref[top + 1 : top + 1 + tiles, cols]
+                u_ref[e, 0, j] = jnp.where(lane >= 3 * LANES // 4, before, here)
+                u_ref[e, 1, j] = jnp.where(lane < LANES // 4, after, here)
+        for r in range(cycles):
+            totals = interpolate(
+                r, cycles, per_dev, u_ref,
+                where_ref[r, 0], where_ref[r, 1], where_ref[r, 2], where_ref[r, 3], tiles,
             )
-            for j in range(cycles):
-                cols = slice(j * LANES, (j + 1) * LANES)
-                here = w_ref[8 : 8 + tiles, cols]
-                u_ref[e, 0, j] = jnp.where(lane >= 3 * LANES // 4, w_ref[7 : 7 + tiles, cols], here)
-                u_ref[e, 1, j] = jnp.where(lane < LANES // 4, w_ref[9 : 9 + tiles, cols], here)
-        for r in range(cycles):
             for e in range(per_dev):
-                maps_ref[r, e] = interpolate(
-                    e, r, cycles, u_ref,
-                    where_ref[r, 0], where_ref[r, 1], where_ref[r, 2], where_ref[r, 3], tiles,
-                )
+                maps_ref[r, e * tiles : (e + 1) * tiles, :] = totals[e]
 
             @pl.when(me != r)
             def _():
@@ -383,19 +413,20 @@
         fin_ref[me] = maps_ref[me]
         for p in peers:
             map_copy(p, p).wait_recv()
-        for s in range(sims):
-            for t in range(tiles):
-                out_ref[s : s + 1, t * LANES : (t + 1) * LANES] = fin_ref[
-                    s // per_dev, s % per_dev, t : t + 1
-                ].astype(jnp.bfloat16)
+        for t in range(tiles):
+            out_ref[:, t * LANES : (t + 1) * LANES] = jnp.concatenate(
+                [fin_ref[h, pl.ds(t, per_dev, stride=tiles), :] for h in range(n_harm)], axis=0
+            ).astype(jnp.bfloat16)
         for p in peers:
             index_copy(me, p).wait_send()
-            order_copy(me, p).wait_send()
             map_copy(me, p).wait_send()
-        for p in [me] + peers:
-            across_copy(q, p).wait_send()
-            sibling_copy(q, p).wait_send()
-            forward_copy(across, p).wait_send()
+        for half in range(2):
+            for p in peers:
+                order_copy(half, me, p).wait_send()
+            for p in [me] + peers:
+                across_copy(half, q, p).wait_send()
+                sibling_copy(half, q, p).wait_send()
+                forward_copy(half, across, p).wait_send()
 
 
 def body(alm, legendre, src_cycle, src_phi, off_cycle, off_phi):
@@ -409,42 +440,46 @@
     tiles = quarter // LANES
     per_group = LANES // cycles
     groups = m_local // per_group
-    piece = per_dev * 2 * cycles
+    turns = groups // 2
+    pairs = cycles // 2
+    piece = per_dev * 2 * pairs
     first_table, twist, second_table = tables(n_harm, n_remap, quarter * n_remap)
     whole = pl.BlockSpec(memory_space=pltpu.VMEM)
-    sems = [pltpu.SemaphoreType.DMA((n_harm,)) for _ in range(12)]
+    single = pltpu.SemaphoreType.DMA((n_harm,))
+    double = pltpu.SemaphoreType.DMA((2, n_harm))
     lensed = pl.pallas_call(
         functools.partial(sky_step, n_harm, n_remap, per_dev),
         grid=(groups,),
         in_specs=[
-            pl.BlockSpec((per_group, 1, rows, depth), lambda g: (0, g, 0, 0)),
-            pl.BlockSpec((per_group, 1, cycles, depth), lambda g: (0, g, 0, 0)),
+            pl.BlockSpec((1, per_group, 1, rows, depth), lambda g: (g // turns, 0, g % turns, 0, 0)),
+            pl.BlockSpec((1, per_group, 1, cycles, depth), lambda g: (g // turns, 0, g % turns, 0, 0)),
         ]
         + [whole] * 7,
         out_specs=whole,
         out_shape=jax.ShapeDtypeStruct((sims, quarter), jnp.bfloat16),
         scratch_shapes=[
-            pltpu.VMEM((rows * cycles, LANES), jnp.float32),
-            pltpu.VMEM((rows * cycles, LANES), jnp.float32),
-            pltpu.VMEM((n_remap * n_harm * piece, LANES), jnp.float32),
+            pltpu.VMEM((rows * pairs, LANES), jnp.float32),
+            pltpu.VMEM((2, rows * pairs, LANES), jnp.float32),
+            pltpu.VMEM((n_remap * n_harm * 2 * piece, LANES), jnp.float32),
             pltpu.VMEM((n_harm, 4, tiles, LANES), jnp.int32),
-            pltpu.VMEM((2, cycles * LANES, 2 * LANES), jnp.bfloat16),
-            pltpu.VMEM((tiles + 16, cycles * LANES), jnp.float32),
+            pltpu.VMEM((2, pairs * LANES, 2 * LANES), jnp.bfloat16),
+            pltpu.VMEM((2 * (tiles + 16), pairs * LANES), jnp.float32),
             pltpu.VMEM((per_dev, 2, cycles, tiles, LANES), jnp.float32),
-            pltpu.VMEM((cycles, per_dev, tiles, LANES), jnp.float32),
-            pltpu.VMEM((n_harm, per_dev, tiles, LANES), jnp.float32),
-        ]
-        + sems,
+            pltpu.VMEM((cycles, per_dev * tiles, LANES), jnp.float32),
+            pltpu.VMEM((n_harm, per_dev * tiles, LANES), jnp.float32),
+            single, single, double, double, double, double,
+            double, double, double, double, single, single,
+        ],
         compiler_params=pltpu.CompilerParams(
             collective_id=0, has_side_effects=True, vmem_limit_bytes=56 * 2**20
         ),
     )(
-        alm.reshape(per_group, groups, rows, depth),
-        legendre.reshape(per_group, groups, cycles, depth),
+        alm.reshape(2, per_group, turns, rows, depth),
+        legendre.reshape(2, per_group, turns, cycles, depth),
         *(array.reshape(tiles, LANES) for array in (src_cycle, src_phi, off_cycle, off_phi)),
-        jnp.asarray(first_table.astype(np.float32)),
+        jnp.asarray(first_table),
         jnp.asarray(twist),
-        jnp.asarray(second_table.astype(np.float32)),
+        jnp.asarray(second_table),
     )
     return lensed.reshape(sims, 1, quarter)
 

time: 41 us -> 41.5 us (1.012)
  Pallas kernels: 39.4 us -> 39.9 us
    pallas_call x1, Pallas kernels: 39.4 us -> 39.9 us  [body(): pl.pallas_call(functools.partial(sky_step, n_harm, n_remap, per_dev), gri...]
where the time goes in v2:
time: 41.5 us; the launch traced here: 41.4 us
  Pallas kernels  39.9 us (96%)
  local copies, waits for them, and re-layouts  1.47 us (4%)
    pallas_call x1, Pallas kernels, body(): pl.pallas_call(functools.partial(sky_step, n_harm, n_remap, per_dev), gri...  39.9 us
    unnamed x1, local copies, waits for them, and re-layouts  1.47 us

profile of v2, /device:TPU:0, one launch (start us, length us, event | category | flops | bytes accessed | tf_op | source)
XLA Modules:
  0.0 41.4 jit_solution(10448445346253457401)
XLA Ops:
  0.0 39.9 %shard_map.91 = bf16[16,2048]{1,0:T(8,128)(2,1)} custom-call(bf16[2,16,4,32,4096]{4,3,2,1,0:T(8,128)(2,1)} %bitcast.7, bf16[2,16,4,8,4096]{4,3,2,1,0:T(8,128)(2,1)} %bitcast.8, s32[16,128]{1,0:T(8,128)} %bitcast.10, s32[16,128]{1,0:T(8,128)} %bitcast.11, s32[16,128]{1,0:T(8,128)} %bitcast.12, s32[16,128]{1,0:T(8,128)} %bitcast.13, ...), custom_call_target="tpu_custom_call" | custom-call | tf_op jit(solution)/shard_map/pallas_call | solution.py:450
  39.9 1.5 %copy.11 = bf16[16,1,2048]{2,0,1:T(8,128)(2,1)} copy(bf16[16,1,2048]{2,0,1:T(8,128)(2,1)} %bitcast.9) | data formatting | bytes 131072

commit v3 on v0

--- a/solution.py
+++ b/solution.py
@@ -1,8 +1,14 @@
 import math
+
+import functools
 
 import jax
 import jax.numpy as jnp
+import ml_dtypes
+import numpy as np
 from jax import lax
+from jax.experimental import pallas as pl
+from jax.experimental.pallas import tpu as pltpu
 from jax.sharding import PartitionSpec as P
 
 DR = 3
@@ -70,7 +76,7 @@
     return jnp.transpose(cycle_values.reshape(cycle_dev, sim_count, count), (1, 0, 2))
 
 
-def body(alm, legendre, src_cycle, src_phi, off_cycle, off_phi):
+def general_body(alm, legendre, src_cycle, src_phi, off_cycle, off_phi):
     sim_count = alm.shape[1] // 2
     n_harm = lax.axis_size("harm")
     n_remap = lax.axis_size("remap")
@@ -116,9 +122,332 @@
     return mixed.reshape(sim_count, cycle_dev, quarter).astype(jnp.bfloat16)
 
 
+LANES = 128
+
+
+def split_bf16(table):
+    high = table.astype(ml_dtypes.bfloat16)
+    low = (table - high.astype(np.float64)).astype(ml_dtypes.bfloat16)
+    return high, low
+
+
+def tables(n_harm, n_remap, phi_count):
+    lane = np.arange(LANES)
+    order = lane % (LANES // 2)
+    parity = lane // (LANES // 2)
+    device = (np.arange(n_harm)[None, :] * n_remap + np.arange(n_remap)[:, None]).reshape(-1)
+    block = (device[:, None] * 2 + np.arange(2)[None, :]).reshape(-1)
+    angle = 2.0 * np.pi * ((np.arange(LANES)[:, None] * block[None, :]) % LANES) / LANES
+    first = np.block([[np.cos(angle), -np.sin(angle)], [np.sin(angle), np.cos(angle)]])
+    high, low = split_bf16(first)
+    first_table = np.concatenate([high, high, low], axis=1).astype(np.float32)
+    angle = 2.0 * np.pi * np.arange(LANES)[:, None] * order[None, :] / phi_count
+    twist = np.stack([np.cos(angle), np.sin(angle)]).astype(np.float32)
+    period = phi_count // LANES
+    rows = np.arange(-8, period + 8) % period
+    angle = 2.0 * np.pi * ((rows[:, None] * order[None, :]) % period) / period
+    second = 2.0 * np.concatenate([np.cos(angle), -np.sin(angle)], axis=1)
+    keep = np.concatenate([parity, parity])[None, None, :] == np.arange(2)[:, None, None]
+    high, low = split_bf16(np.where(keep, second[None], 0.0))
+    second_table = np.concatenate([high, low]).astype(np.float32)
+    return first_table, twist, second_table
+
+
+def dot_last(a, b):
+    return lax.dot_general(a, b, (((1,), (1,)), ((), ())), preferred_element_type=jnp.float32)
+
+
+def synthesize_sim(x_ref, e, step, pairs, first, twist_ref, second, z_ref):
+    blocks = x_ref.shape[0] // step
+    columns = []
+    for pair in range(pairs):
+        columns.append(
+            jnp.concatenate(
+                [
+                    x_ref[pl.ds((e * 2 + c) * pairs + pair, blocks, stride=step), :]
+                    for c in range(2)
+                ],
+                axis=0,
+            )
+        )
+    coeffs = jnp.concatenate(columns, axis=1)
+    high = coeffs.astype(jnp.bfloat16)
+    low = (coeffs - high.astype(jnp.float32)).astype(jnp.bfloat16)
+    section = jnp.dot(
+        first, jnp.concatenate([high, low, high], axis=0), preferred_element_type=jnp.float32
+    )
+    for pair in range(pairs):
+        cols = slice(pair * LANES, (pair + 1) * LANES)
+        re = section[:LANES, cols]
+        im = section[LANES:, cols]
+        turned = jnp.concatenate(
+            [
+                re * twist_ref[0] - im * twist_ref[1],
+                re * twist_ref[1] + im * twist_ref[0],
+            ],
+            axis=1,
+        )
+        turned_high = turned.astype(jnp.bfloat16)
+        z_ref[0, cols, :] = turned_high
+        z_ref[1, cols, :] = (turned - turned_high.astype(jnp.float32)).astype(jnp.bfloat16)
+    span = second.shape[0] // 2
+    both = dot_last(second, z_ref[0])
+    return both[:span] + both[span:] + dot_last(second[:span], z_ref[1])
+
+
+def interpolate(r, cycles, per_dev, u_ref, sc, sp, oc, op, tiles):
+    lane = lax.broadcasted_iota(jnp.int32, (tiles, LANES), 1)
+    near_index = sp & (LANES - 1)
+    far_index = (sp + 1) & (LANES - 1)
+    b = op.astype(jnp.float32) * (1.0 / QF)
+    a = oc.astype(jnp.float32) * (1.0 / QF)
+    totals = [jnp.zeros((tiles, LANES), jnp.float32) for _ in range(per_dev)]
+    for j in range(max(0, r - DR), min(cycles - 1, r + DR) + 1):
+        weight = jnp.where(sc == j, 1.0 - a, jnp.where(sc == j - 1, a, 0.0))
+        near_weight = weight * (1.0 - b)
+        far_weight = weight * b
+        for e in range(per_dev):
+            left = u_ref[e, 0, j]
+            right = u_ref[e, 1, j]
+            near, far = (
+                jnp.where(
+                    lane < LANES // 2,
+                    jnp.take_along_axis(left, index, axis=1, mode="promise_in_bounds"),
+                    jnp.take_along_axis(right, index, axis=1, mode="promise_in_bounds"),
+                )
+                for index in (near_index, far_index)
+            )
+            totals[e] = totals[e] + near_weight * near + far_weight * far
+    return totals
+
+
+def to_device(src, dst, send_sem, recv_sem, axis, index):
+    return pltpu.make_async_remote_copy(
+        src_ref=src,
+        dst_ref=dst,
+        send_sem=send_sem,
+        recv_sem=recv_sem,
+        device_id={axis: index},
+        device_id_type=pl.DeviceIdType.MESH,
+    )
+
+
+def sky_step(
+    n_harm, n_remap, per_dev,
+    sums_ref, sc_ref, sp_ref, oc_ref, op_ref, first_ref, twist_ref, second_ref,
+    out_ref,
+    half_ref, pack_ref, x_ref, z_ref, w_ref, u_ref, maps_ref, fin_ref,
+    a_send, a_recv, y_send, y_recv, s_send, s_recv, f_send, f_recv, o_send, o_recv,
+):
+    cycles, rows, _ = sums_ref.shape
+    pairs = cycles // 2
+    tiles = sc_ref.shape[1]
+    sims = rows // 2
+    half_piece = per_dev * 2 * pairs
+    piece = 2 * half_piece
+    me = lax.axis_index("harm")
+    q = lax.axis_index("remap")
+    across = lax.rem(q + 2, n_remap)
+    sibling = q + 1 - 2 * lax.rem(q, 2)
+    far = lax.rem(sibling + 2, n_remap)
+    peers = [lax.rem(me + k, n_harm) for k in range(1, n_harm)]
+
+    def slot(quarter, source):
+        start = pl.multiple_of((quarter * n_harm + source) * piece, piece)
+        return x_ref.at[pl.ds(start, piece), :]
+
+    def packed(target):
+        return pack_ref.at[pl.ds(pl.multiple_of(target * piece, piece), piece), :]
+
+    def order_copy(source, target):
+        return to_device(
+            packed(target), slot(q, source), a_send.at[target], a_recv.at[source], "harm", target
+        )
+
+    def across_copy(quarter, source):
+        held = slot(quarter, source)
+        return to_device(held, held, y_send.at[source], y_recv.at[source], "remap", across)
+
+    def sibling_copy(quarter, source):
+        held = slot(quarter, source)
+        return to_device(held, held, s_send.at[source], s_recv.at[source], "remap", sibling)
+
+    def forward_copy(quarter, source):
+        held = slot(quarter, source)
+        return to_device(held, held, f_send.at[source], f_recv.at[source], "remap", sibling)
+
+    def map_copy(source, target):
+        return to_device(
+            maps_ref.at[target], fin_ref.at[source], o_send.at[target], o_recv.at[source], "harm", target
+        )
+
+    barrier = pltpu.get_barrier_semaphore()
+    for p in peers:
+        pl.semaphore_signal(
+            barrier, inc=1, device_id={"harm": p}, device_id_type=pl.DeviceIdType.MESH
+        )
+    for p in (across, sibling):
+        pl.semaphore_signal(
+            barrier, inc=1, device_id={"remap": p}, device_id_type=pl.DeviceIdType.MESH
+        )
+    device = me * n_remap + q
+    row_lane = lax.broadcasted_iota(jnp.int32, (rows, LANES), 1)
+    for pair in range(pairs):
+        even, odd = sums_ref[2 * pair], sums_ref[2 * pair + 1]
+        zero_order = jnp.logical_and(device == 0, row_lane == 0)
+        even = jnp.where(zero_order, 0.5 * even, even)
+        odd = jnp.where(zero_order, 0.5 * odd, odd)
+        half_ref[pair * rows : (pair + 1) * rows, :] = jnp.where(
+            row_lane < LANES // 2, even, pltpu.roll(odd, LANES // 2, axis=1)
+        )
+        half_ref[(pairs + pair) * rows : (pairs + pair + 1) * rows, :] = jnp.where(
+            row_lane < LANES // 2, pltpu.roll(even, LANES // 2, axis=1), odd
+        )
+    for half in range(2):
+        for k in range(rows):
+            sim, part = k % sims, k // sims
+            start = (sim // per_dev) * piece + half * half_piece
+            start += ((sim % per_dev) * 2 + part) * pairs
+            pack_ref[start : start + pairs, :] = half_ref[
+                pl.ds(half * pairs * rows + k, pairs, stride=rows), :
+            ]
+    pl.semaphore_wait(barrier, n_harm + 1)
+    for p in peers:
+        order_copy(me, p).start()
+    own = pl.multiple_of((q * n_harm + me) * piece, piece)
+    x_ref[pl.ds(own, piece), :] = pack_ref[pl.ds(pl.multiple_of(me * piece, piece), piece), :]
+    across_copy(q, me).start()
+    sibling_copy(q, me).start()
+    for p in peers:
+        order_copy(p, p).wait_recv()
+        across_copy(q, p).start()
+        sibling_copy(q, p).start()
+    for p in [me] + peers:
+        across_copy(across, p).wait_recv()
+        forward_copy(across, p).start()
+    for p in [me] + peers:
+        sibling_copy(sibling, p).wait_recv()
+        forward_copy(far, p).wait_recv()
+
+    start = pl.multiple_of(q * tiles, tiles)
+    span = tiles + 16
+    second = jnp.concatenate(
+        [second_ref[i, pl.ds(start, span), :] for i in range(4)], axis=0
+    ).astype(jnp.bfloat16)
+    first = first_ref[...].astype(jnp.bfloat16)
+    lane = lax.broadcasted_iota(jnp.int32, (tiles, LANES), 1)
+    for e in range(per_dev):
+        w_ref[...] = synthesize_sim(x_ref, e, half_piece, pairs, first, twist_ref, second, z_ref)
+        for j in range(cycles):
+            cols = slice((j // 2) * LANES, (j // 2 + 1) * LANES)
+            top = (j % 2) * span + 8
+            here = w_ref[top : top + tiles, cols]
+            before = w_ref[top - 1 : top - 1 + tiles, cols]
+            after = w_ref[top + 1 : top + 1 + tiles, cols]
+            u_ref[e, 0, j] = jnp.where(lane >= 3 * LANES // 4, before, here)
+            u_ref[e, 1, j] = jnp.where(lane < LANES // 4, after, here)
+    for r in range(cycles):
+        totals = interpolate(
+            r, cycles, per_dev, u_ref,
+            sc_ref[r], sp_ref[r], oc_ref[r], op_ref[r], tiles,
+        )
+        for e in range(per_dev):
+            maps_ref[r, e * tiles : (e + 1) * tiles, :] = totals[e]
+
+        @pl.when(me != r)
+        def _():
+            map_copy(me, r).start()
+
+    fin_ref[me] = maps_ref[me]
+    for p in peers:
+        map_copy(p, p).wait_recv()
+    for t in range(tiles):
+        out_ref[:, t * LANES : (t + 1) * LANES] = jnp.concatenate(
+            [fin_ref[h, pl.ds(t, per_dev, stride=tiles), :] for h in range(n_harm)], axis=0
+        ).astype(jnp.bfloat16)
+    for p in peers:
+        order_copy(me, p).wait_send()
+        map_copy(me, p).wait_send()
+    for p in [me] + peers:
+        across_copy(q, p).wait_send()
+        sibling_copy(q, p).wait_send()
+        forward_copy(across, p).wait_send()
+
+
+def body(alm, legendre, src_cycle, src_phi, off_cycle, off_phi):
+    n_harm = lax.axis_size("harm")
+    n_remap = lax.axis_size("remap")
+    rows = alm.shape[1]
+    sims = rows // 2
+    per_dev = sims // n_harm
+    cycles = legendre.shape[1]
+    quarter = src_cycle.shape[1]
+    tiles = quarter // LANES
+    pairs = cycles // 2
+    piece = per_dev * 4 * pairs
+    first_table, twist, second_table = tables(n_harm, n_remap, quarter * n_remap)
+    where = [
+        lax.all_gather(array, "harm", axis=0, tiled=True).reshape(cycles, tiles, LANES)
+        for array in (src_cycle, src_phi, off_cycle, off_phi)
+    ]
+    sums = jnp.einsum("mkl,mrl->rkm", alm, legendre, preferred_element_type=jnp.float32)
+    whole = pl.BlockSpec(memory_space=pltpu.VMEM)
+    lensed = pl.pallas_call(
+        functools.partial(sky_step, n_harm, n_remap, per_dev),
+        in_specs=[whole] * 8,
+        out_specs=whole,
+        out_shape=jax.ShapeDtypeStruct((sims, quarter), jnp.bfloat16),
+        scratch_shapes=[
+            pltpu.VMEM((rows * 2 * pairs, LANES), jnp.float32),
+            pltpu.VMEM((rows * 2 * pairs, LANES), jnp.float32),
+            pltpu.VMEM((n_remap * n_harm * piece, LANES), jnp.float32),
+            pltpu.VMEM((2, pairs * LANES, 2 * LANES), jnp.bfloat16),
+            pltpu.VMEM((2 * (tiles + 16), pairs * LANES), jnp.float32),
+            pltpu.VMEM((per_dev, 2, cycles, tiles, LANES), jnp.float32),
+            pltpu.VMEM((cycles, per_dev * tiles, LANES), jnp.float32),
+            pltpu.VMEM((n_harm, per_dev * tiles, LANES), jnp.float32),
+        ]
+        + [pltpu.SemaphoreType.DMA((n_harm,)) for _ in range(10)],
+        compiler_params=pltpu.CompilerParams(
+            collective_id=0, has_side_effects=True, vmem_limit_bytes=16 * 2**20
+        ),
+    )(
+        sums,
+        *where,
+        jnp.asarray(first_table),
+        jnp.asarray(twist),
+        jnp.asarray(second_table),
+    )
+    return lensed.reshape(sims, 1, quarter)
+
+
+def fits(mesh, alm, legendre, src_cycle):
+    n_harm, n_remap = mesh.shape["harm"], mesh.shape["remap"]
+    cycles = legendre.shape[1]
+    sims = alm.shape[1] // 2
+    phi_count = src_cycle.shape[1]
+    return (
+        cycles == n_harm == 8
+        and sims % n_harm == 0
+        and alm.shape[0] == LANES * n_harm * n_remap
+        and phi_count == LANES * 64
+        and (phi_count // n_remap) % (16 * LANES) == 0
+        and (n_harm * n_remap) % 8 == 0
+        and n_remap == 4
+    )
+
+
 def solution(mesh):
+    def run(*arrays):
+        chosen = body if fits(mesh, arrays[0], arrays[1], arrays[2]) else general_body
+        return sharded(mesh, chosen)(*arrays)
+
+    return run
+
+
+def sharded(mesh, chosen):
     return jax.shard_map(
-        body,
+        chosen,
         mesh=mesh,
         in_specs=(
             P(("harm", "remap"), None, None),

time: 146 us -> 161 us (1.10)
  the two profiles are of different devices: /device:TPU:2 before, /device:TPU:0 now
where the time goes in v3:
time: 161 us
  blocking collectives  124 us (77%)
  Pallas kernels  19.8 us (12%)
  matrix products  16.6 us (10%)
    all_gather x4, blocking collectives, body(): lax.all_gather(array, 'harm', axis=0, tiled=True)  124 us
    pallas_call x1, Pallas kernels, body(): pl.pallas_call(functools.partial(sky_step, n_harm, n_remap, per_dev), in_...  19.8 us
    dot_general x1, matrix products, body(): jnp.einsum('mkl,mrl->rkm', alm, legendre, preferred_element_type=jnp.floa...  16.6 us

profile of v3, /device:TPU:0, one launch (start us, length us, event | category | flops | bytes accessed | tf_op | source)
XLA Modules:
  0.0 161.0 jit_solution(10838277782548419426)
XLA Ops:
  0.0 0.0 copy-start
  0.0 0.0 copy-start.2
  0.0 0.0 copy-start.1
  0.0 0.0 copy-start.3
  0.0 0.0 copy-start.4
  0.0 0.0 copy-start.5
  0.0 0.0 copy-start.6
  0.0 16.6 %fusion = f32[128,8,32]{2,1,0:T(8,128)S(1)} fusion(bf16[128,8,4096]{2,1,0:T(8,128)(2,1)} %param.10, bf16[128,32,4096]{2,1,0:T(8,128)(2,1)} %param.9), kind=kOutput, calls=%fused_computation | convolution fusion | flops 268435456 | bytes 42074112 | tf_op jit(solution)/shard_map/mkl,mrl->rkm/dot_general | solution.py:393
  16.6 0.2 copy.11
  16.8 0.0 copy-done.3
  16.8 32.3 %all-gather = s32[8,1,2048]{2,1,0:T(1,128)S(1)} all-gather(s32[1,1,2048]{2,1,0:T(1,128)S(1)} %bitcast.18), channel_id=1, replica_groups=mesh['harm'=8,'remap'=4] {'harm'}, dimensions={0}, use_global_device_ids=true | all-gather | bytes 73728 | tf_op jit(solution)/shard_map/all_gather | solution.py:390
  49.1 0.0 copy-done.4
  49.1 30.5 %all-gather.1 = s32[8,1,2048]{2,1,0:T(1,128)S(1)} all-gather(s32[1,1,2048]{2,1,0:T(1,128)S(1)} %bitcast.19), channel_id=1, replica_groups=mesh['harm'=8,'remap'=4] {'harm'}, dimensions={0}, use_global_device_ids=true | all-gather | bytes 73728 | tf_op jit(solution)/shard_map/all_gather | solution.py:390
  79.6 0.0 copy-done.5
  79.6 30.5 %all-gather.2 = s32[8,1,2048]{2,1,0:T(1,128)S(1)} all-gather(s32[1,1,2048]{2,1,0:T(1,128)S(1)} %bitcast.20), channel_id=1, replica_groups=mesh['harm'=8,'remap'=4] {'harm'}, dimensions={0}, use_global_device_ids=true | all-gather | bytes 73728 | tf_op jit(solution)/shard_map/all_gather | solution.py:390
  110.1 0.0 copy-done.6
  110.1 30.5 %all-gather.3 = s32[8,1,2048]{2,1,0:T(1,128)S(1)} all-gather(s32[1,1,2048]{2,1,0:T(1,128)S(1)} %bitcast.21), channel_id=1, replica_groups=mesh['harm'=8,'remap'=4] {'harm'}, dimensions={0}, use_global_device_ids=true | all-gather | bytes 73728 | tf_op jit(solution)/shard_map/all_gather | solution.py:390
  140.6 0.0 copy-done
  140.6 0.0 copy-done.2
  140.6 0.0 copy-done.1
  140.6 19.8 %shard_map.91 = bf16[16,2048]{1,0:T(8,128)(2,1)S(1)} custom-call(f32[8,32,128]{2,1,0:T(8,128)S(1)} %bitcast.12, s32[8,16,128]{2,1,0:T(8,128)S(1)} %bitcast.14, s32[8,16,128]{2,1,0:T(8,128)S(1)} %bitcast.15, s32[8,16,128]{2,1,0:T(8,128)S(1)} %bitcast.16, s32[8,16,128]{2,1,0:T(8,128)S(1)} %bitcast.17, f32[256,384]{1,0:T(8,128)S(1)} %copy-done, ...), custom_call_target="tpu_custom_call" | custom-call | tf_op jit(solution)/shard_map/pallas_call | solution.py:395
  160.4 0.6 copy.13
Async XLA Ops:
  0.0 140.6 %copy-start = (f32[256,384]{1,0:T(8,128)S(1)}, f32[256,384]{1,0:T(8,128)}, u32[]{:S(2)}) copy-start(f32[256,384]{1,0:T(8,128)} %constant.6.clone.first_ref) | copy-start | bytes 1179652
  0.0 140.6 %copy-start.2 = (f32[2,128,128]{2,1,0:T(8,128)S(1)}, f32[2,128,128]{2,1,0:T(8,128)}, u32[]{:S(2)}) copy-start(f32[2,128,128]{2,1,0:T(8,128)} %constant.7.clone.twist_ref) | copy-start | bytes 393220
  0.0 140.6 %copy-start.1 = (f32[4,80,256]{2,1,0:T(8,128)S(1)}, f32[4,80,256]{2,1,0:T(8,128)}, u32[]{:S(2)}) copy-start(f32[4,80,256]{2,1,0:T(8,128)} %constant.8.clone.second_ref) | copy-start | bytes 983044
  0.0 16.8 %copy-start.3 = (s32[1,2048]{1,0:T(1,128)S(1)}, s32[1,2048]{1,0:T(1,128)}, u32[]{:S(2)}) copy-start(s32[1,2048]{1,0:T(1,128)} %param.11) | copy-start | bytes 24580
  0.0 49.1 %copy-start.4 = (s32[1,2048]{1,0:T(1,128)S(1)}, s32[1,2048]{1,0:T(1,128)}, u32[]{:S(2)}) copy-start(s32[1,2048]{1,0:T(1,128)} %param.12) | copy-start | bytes 24580
  0.0 79.6 %copy-start.5 = (s32[1,2048]{1,0:T(1,128)S(1)}, s32[1,2048]{1,0:T(1,128)}, u32[]{:S(2)}) copy-start(s32[1,2048]{1,0:T(1,128)} %param.13) | copy-start | bytes 24580
  0.0 110.1 %copy-start.6 = (s32[1,2048]{1,0:T(1,128)S(1)}, s32[1,2048]{1,0:T(1,128)}, u32[]{:S(2)}) copy-start(s32[1,2048]{1,0:T(1,128)} %param.14) | copy-start | bytes 24580

commit v4 on v2

--- a/solution.py
+++ b/solution.py
@@ -153,28 +153,45 @@
     return first_table, twist, second_table
 
 
-def accumulate_orders(half, turn, alm_ref, leg_ref, acc_ref):
-    _, per_group, _, rows, depth = alm_ref.shape
-    cycles = leg_ref.shape[3]
+def accumulate_orders(turn, alm_ref, leg_ref, rows_ref):
+    per_group, rows, depth = alm_ref.shape
+    cycles = leg_ref.shape[1]
+    share = LANES // rows
     coeffs = alm_ref[...].reshape(per_group * rows, depth)
     basis = leg_ref[...].reshape(per_group * cycles, depth)
-    product = lax.dot_general(
-        coeffs, basis, (((1,), (1,)), ((), ())), preferred_element_type=jnp.float32
-    )
+    product = dot_last(basis, coeffs)
+    lane = lax.broadcasted_iota(jnp.int32, (cycles, LANES), 1)
+    parts = []
+    for t in range(per_group // share):
+        cols = slice(t * LANES, (t + 1) * LANES)
+        own = jnp.zeros((cycles, LANES), jnp.float32)
+        for i in range(share):
+            top = (t * share + i) * cycles
+            own = jnp.where(lane // rows == i, product[top : top + cycles, cols], own)
+        parts.append(own)
+    block = jnp.concatenate(parts, axis=0)
+    height = block.shape[0]
+    rows_ref[pl.ds(pl.multiple_of(turn * height, height), height), :] = block
+
+
+def arrange_orders(half, rows, cycles, rows_ref, acc_ref):
+    turned_rows = rows_ref[...].T
     lane = lax.broadcasted_iota(jnp.int32, (rows, LANES), 1)
-    own = jnp.zeros((rows, LANES), jnp.float32)
-    for i in range(per_group):
-        own = jnp.where(lane // cycles == i, product[i * rows : (i + 1) * rows], own)
     device = lax.axis_index("harm") * lax.axis_size("remap") + lax.axis_index("remap")
-    first_order = jnp.logical_and(device == 0, jnp.logical_and(half == 0, turn == 0))
-    for r in range(cycles):
-        place = 4 * (r % 2) + turn
-        turned = pltpu.roll(own, lax.rem(place - r + LANES, LANES), axis=1)
-        turned = jnp.where(jnp.logical_and(first_order, lane == place), 0.5 * turned, turned)
-        at = (r // 2) * rows
-        acc_ref[at : at + rows, :] = jnp.where(
-            lane % cycles == place, turned, acc_ref[at : at + rows, :]
-        )
+    first_order = jnp.logical_and(device == 0, half == 0)
+    for pair in range(cycles // 2):
+        total = jnp.zeros((rows, LANES), jnp.float32)
+        for low in range(2):
+            for i in range(LANES // rows):
+                place, r = 4 * low + i, 2 * pair + low
+                turned = pltpu.roll(
+                    turned_rows[i * rows : (i + 1) * rows], (place - r) % LANES, axis=1
+                )
+                if i == 0:
+                    zero = jnp.logical_and(first_order, lane == place)
+                    turned = jnp.where(zero, 0.5 * turned, turned)
+                total = jnp.where(lane % cycles == place, turned, total)
+        acc_ref[pair * rows : (pair + 1) * rows, :] = total
 
 
 def dot_last(a, b):
@@ -260,16 +277,16 @@
     n_harm, n_remap, per_dev,
     alm_ref, leg_ref, sc_ref, sp_ref, oc_ref, op_ref, first_ref, twist_ref, second_ref,
     out_ref,
-    acc_ref, pack_ref, x_ref, where_ref, z_ref, w_ref, u_ref, maps_ref, fin_ref,
+    rows_ref, acc_ref, pack_ref, x_ref, where_ref, z_ref, w_ref, u_ref, maps_ref, fin_ref,
     i_send, i_recv, a_send, a_recv, y_send, y_recv, s_send, s_recv, f_send, f_recv, o_send, o_recv,
 ):
     group = pl.program_id(0)
     groups = pl.num_programs(0)
     turns = groups // 2
-    cycles = leg_ref.shape[3]
+    cycles = leg_ref.shape[1]
     pairs = cycles // 2
     tiles = sc_ref.shape[0]
-    rows = alm_ref.shape[3]
+    rows = alm_ref.shape[1]
     sims = rows // 2
     piece = per_dev * 2 * pairs
     me = lax.axis_index("harm")
@@ -315,6 +332,7 @@
         )
 
     def send_orders(half):
+        arrange_orders(half, rows, cycles, rows_ref, acc_ref)
         for k in range(rows):
             sim, part = k % sims, k // sims
             start = (sim // per_dev) * piece + ((sim % per_dev) * 2 + part) * pairs
@@ -355,7 +373,7 @@
         for p in peers:
             index_copy(me, p).start()
 
-    accumulate_orders(group // turns, lax.rem(group, turns), alm_ref, leg_ref, acc_ref)
+    accumulate_orders(lax.rem(group, turns), alm_ref, leg_ref, rows_ref)
 
     @pl.when(group == turns - 1)
     def _():
@@ -440,7 +458,6 @@
     tiles = quarter // LANES
     per_group = LANES // cycles
     groups = m_local // per_group
-    turns = groups // 2
     pairs = cycles // 2
     piece = per_dev * 2 * pairs
     first_table, twist, second_table = tables(n_harm, n_remap, quarter * n_remap)
@@ -451,13 +468,14 @@
         functools.partial(sky_step, n_harm, n_remap, per_dev),
         grid=(groups,),
         in_specs=[
-            pl.BlockSpec((1, per_group, 1, rows, depth), lambda g: (g // turns, 0, g % turns, 0, 0)),
-            pl.BlockSpec((1, per_group, 1, cycles, depth), lambda g: (g // turns, 0, g % turns, 0, 0)),
+            pl.BlockSpec((per_group, rows, depth), lambda g: (g, 0, 0)),
+            pl.BlockSpec((per_group, cycles, depth), lambda g: (g, 0, 0)),
         ]
         + [whole] * 7,
         out_specs=whole,
         out_shape=jax.ShapeDtypeStruct((sims, quarter), jnp.bfloat16),
         scratch_shapes=[
+            pltpu.VMEM((LANES, LANES), jnp.float32),
             pltpu.VMEM((rows * pairs, LANES), jnp.float32),
             pltpu.VMEM((2, rows * pairs, LANES), jnp.float32),
             pltpu.VMEM((n_remap * n_harm * 2 * piece, LANES), jnp.float32),
@@ -474,8 +492,8 @@
             collective_id=0, has_side_effects=True, vmem_limit_bytes=56 * 2**20
         ),
     )(
-        alm.reshape(2, per_group, turns, rows, depth),
-        legendre.reshape(2, per_group, turns, cycles, depth),
+        alm,
+        legendre,
         *(array.reshape(tiles, LANES) for array in (src_cycle, src_phi, off_cycle, off_phi)),
         jnp.asarray(first_table),
         jnp.asarray(twist),
@@ -491,6 +509,7 @@
     phi_count = src_cycle.shape[1]
     return (
         cycles == n_harm == 8
+        and alm.shape[1] == 32
         and sims % n_harm == 0
         and alm.shape[0] == LANES * n_harm * n_remap
         and phi_count == LANES * 64

time: 41.5 us -> 42.5 us (1.024)
  Pallas kernels: 39.9 us -> 40.8 us
    pallas_call x1, Pallas kernels: 39.9 us -> 40.8 us  [body(): pl.pallas_call(functools.partial(sky_step, n_harm, n_remap, per_dev), gri...]
where the time goes in v4:
time: 42.5 us; the launch traced here: 42.3 us
  Pallas kernels  40.8 us (96%)
  local copies, waits for them, and re-layouts  1.47 us (3%)
    pallas_call x1, Pallas kernels, body(): pl.pallas_call(functools.partial(sky_step, n_harm, n_remap, per_dev), gri...  40.8 us
    unnamed x1, local copies, waits for them, and re-layouts  1.47 us

profile of v4, /device:TPU:0, one launch (start us, length us, event | category | flops | bytes accessed | tf_op | source)
XLA Modules:
  0.0 42.3 jit_solution(3939406728460648757)
XLA Ops:
  0.0 40.8 %shard_map.91 = bf16[16,2048]{1,0:T(8,128)(2,1)} custom-call(bf16[128,32,4096]{2,1,0:T(8,128)(2,1)} %alm_ref.1, bf16[128,8,4096]{2,1,0:T(8,128)(2,1)} %leg_ref.1, s32[16,128]{1,0:T(8,128)} %bitcast.6, s32[16,128]{1,0:T(8,128)} %bitcast.7, s32[16,128]{1,0:T(8,128)} %bitcast.8, s32[16,128]{1,0:T(8,128)} %bitcast.9, f32[256,384]{1,0:T(8,128)} %constant.6.clone.first_ref, ...), custom_call_target="tpu_custom_call" | custom-call | tf_op jit(solution)/shard_map/pallas_call | solution.py:467
  40.8 1.5 %copy.11 = bf16[16,1,2048]{2,0,1:T(8,128)(2,1)} copy(bf16[16,1,2048]{2,0,1:T(8,128)(2,1)} %bitcast.5) | data formatting | bytes 131072

commit v5 on v3

--- a/solution.py
+++ b/solution.py
@@ -195,30 +195,27 @@
     return both[:span] + both[span:] + dot_last(second[:span], z_ref[1])
 
 
-def interpolate(r, cycles, per_dev, u_ref, sc, sp, oc, op, tiles):
+def interpolate(r, cycles, e, u_ref, sc, sp, oc, op, tiles):
     lane = lax.broadcasted_iota(jnp.int32, (tiles, LANES), 1)
     near_index = sp & (LANES - 1)
     far_index = (sp + 1) & (LANES - 1)
     b = op.astype(jnp.float32) * (1.0 / QF)
     a = oc.astype(jnp.float32) * (1.0 / QF)
-    totals = [jnp.zeros((tiles, LANES), jnp.float32) for _ in range(per_dev)]
+    total = jnp.zeros((tiles, LANES), jnp.float32)
     for j in range(max(0, r - DR), min(cycles - 1, r + DR) + 1):
         weight = jnp.where(sc == j, 1.0 - a, jnp.where(sc == j - 1, a, 0.0))
-        near_weight = weight * (1.0 - b)
-        far_weight = weight * b
-        for e in range(per_dev):
-            left = u_ref[e, 0, j]
-            right = u_ref[e, 1, j]
-            near, far = (
-                jnp.where(
-                    lane < LANES // 2,
-                    jnp.take_along_axis(left, index, axis=1, mode="promise_in_bounds"),
-                    jnp.take_along_axis(right, index, axis=1, mode="promise_in_bounds"),
-                )
-                for index in (near_index, far_index)
+        left = u_ref[e, 0, j]
+        right = u_ref[e, 1, j]
+        near, far = (
+            jnp.where(
+                lane < LANES // 2,
+                jnp.take_along_axis(left, index, axis=1, mode="promise_in_bounds"),
+                jnp.take_along_axis(right, index, axis=1, mode="promise_in_bounds"),
             )
-            totals[e] = totals[e] + near_weight * near + far_weight * far
-    return totals
+            for index in (near_index, far_index)
+        )
+        total = total + weight * ((1.0 - b) * near + b * far)
+    return total
 
 
 def to_device(src, dst, send_sem, recv_sem, axis, index):
@@ -236,12 +233,12 @@
     n_harm, n_remap, per_dev,
     sums_ref, sc_ref, sp_ref, oc_ref, op_ref, first_ref, twist_ref, second_ref,
     out_ref,
-    half_ref, pack_ref, x_ref, z_ref, w_ref, u_ref, maps_ref, fin_ref,
-    a_send, a_recv, y_send, y_recv, s_send, s_recv, f_send, f_recv, o_send, o_recv,
+    half_ref, pack_ref, x_ref, where_ref, z_ref, w_ref, u_ref, maps_ref, fin_ref,
+    i_send, i_recv, a_send, a_recv, y_send, y_recv, s_send, s_recv, f_send, f_recv, o_send, o_recv,
 ):
     cycles, rows, _ = sums_ref.shape
     pairs = cycles // 2
-    tiles = sc_ref.shape[1]
+    tiles = sc_ref.shape[0]
     sims = rows // 2
     half_piece = per_dev * 2 * pairs
     piece = 2 * half_piece
@@ -276,10 +273,16 @@
         held = slot(quarter, source)
         return to_device(held, held, f_send.at[source], f_recv.at[source], "remap", sibling)
 
-    def map_copy(source, target):
+    def map_copy(e, source, target):
+        part = pl.ds(e * tiles, tiles)
         return to_device(
-            maps_ref.at[target], fin_ref.at[source], o_send.at[target], o_recv.at[source], "harm", target
-        )
+            maps_ref.at[target, part], fin_ref.at[source, part],
+            o_send.at[e, target], o_recv.at[e, source], "harm", target,
+        )
+
+    def index_copy(source, target):
+        held = where_ref.at[source]
+        return to_device(held, held, i_send.at[target], i_recv.at[source], "harm", target)
 
     barrier = pltpu.get_barrier_semaphore()
     for p in peers:
@@ -290,6 +293,8 @@
         pl.semaphore_signal(
             barrier, inc=1, device_id={"remap": p}, device_id_type=pl.DeviceIdType.MESH
         )
+    for i, ref in enumerate((sc_ref, sp_ref, oc_ref, op_ref)):
+        where_ref[me, i] = ref[...]
     device = me * n_remap + q
     row_lane = lax.broadcasted_iota(jnp.int32, (rows, LANES), 1)
     for pair in range(pairs):
@@ -318,6 +323,8 @@
     x_ref[pl.ds(own, piece), :] = pack_ref[pl.ds(pl.multiple_of(me * piece, piece), piece), :]
     across_copy(q, me).start()
     sibling_copy(q, me).start()
+    for p in peers:
+        index_copy(me, p).start()
     for p in peers:
         order_copy(p, p).wait_recv()
         across_copy(q, p).start()
@@ -346,28 +353,32 @@
             after = w_ref[top + 1 : top + 1 + tiles, cols]
             u_ref[e, 0, j] = jnp.where(lane >= 3 * LANES // 4, before, here)
             u_ref[e, 1, j] = jnp.where(lane < LANES // 4, after, here)
-    for r in range(cycles):
-        totals = interpolate(
-            r, cycles, per_dev, u_ref,
-            sc_ref[r], sp_ref[r], oc_ref[r], op_ref[r], tiles,
-        )
-        for e in range(per_dev):
-            maps_ref[r, e * tiles : (e + 1) * tiles, :] = totals[e]
-
-        @pl.when(me != r)
-        def _():
-            map_copy(me, r).start()
+        if e == 0:
+            for p in peers:
+                index_copy(p, p).wait_recv()
+        for r in range(cycles):
+            maps_ref[r, e * tiles : (e + 1) * tiles, :] = interpolate(
+                r, cycles, e, u_ref,
+                where_ref[r, 0], where_ref[r, 1], where_ref[r, 2], where_ref[r, 3], tiles,
+            )
+
+            @pl.when(me != r)
+            def _(e=e, r=r):
+                map_copy(e, me, r).start()
 
     fin_ref[me] = maps_ref[me]
-    for p in peers:
-        map_copy(p, p).wait_recv()
+    for e in range(per_dev):
+        for p in peers:
+            map_copy(e, p, p).wait_recv()
     for t in range(tiles):
         out_ref[:, t * LANES : (t + 1) * LANES] = jnp.concatenate(
             [fin_ref[h, pl.ds(t, per_dev, stride=tiles), :] for h in range(n_harm)], axis=0
         ).astype(jnp.bfloat16)
     for p in peers:
+        index_copy(me, p).wait_send()
         order_copy(me, p).wait_send()
-        map_copy(me, p).wait_send()
+        for e in range(per_dev):
+            map_copy(e, me, p).wait_send()
     for p in [me] + peers:
         across_copy(q, p).wait_send()
         sibling_copy(q, p).wait_send()
@@ -386,10 +397,7 @@
     pairs = cycles // 2
     piece = per_dev * 4 * pairs
     first_table, twist, second_table = tables(n_harm, n_remap, quarter * n_remap)
-    where = [
-        lax.all_gather(array, "harm", axis=0, tiled=True).reshape(cycles, tiles, LANES)
-        for array in (src_cycle, src_phi, off_cycle, off_phi)
-    ]
+    where = [array.reshape(tiles, LANES) for array in (src_cycle, src_phi, off_cycle, off_phi)]
     sums = jnp.einsum("mkl,mrl->rkm", alm, legendre, preferred_element_type=jnp.float32)
     whole = pl.BlockSpec(memory_space=pltpu.VMEM)
     lensed = pl.pallas_call(
@@ -401,13 +409,15 @@
             pltpu.VMEM((rows * 2 * pairs, LANES), jnp.float32),
             pltpu.VMEM((rows * 2 * pairs, LANES), jnp.float32),
             pltpu.VMEM((n_remap * n_harm * piece, LANES), jnp.float32),
+            pltpu.VMEM((n_harm, 4, tiles, LANES), jnp.int32),
             pltpu.VMEM((2, pairs * LANES, 2 * LANES), jnp.bfloat16),
             pltpu.VMEM((2 * (tiles + 16), pairs * LANES), jnp.float32),
             pltpu.VMEM((per_dev, 2, cycles, tiles, LANES), jnp.float32),
             pltpu.VMEM((cycles, per_dev * tiles, LANES), jnp.float32),
             pltpu.VMEM((n_harm, per_dev * tiles, LANES), jnp.float32),
         ]
-        + [pltpu.SemaphoreType.DMA((n_harm,)) for _ in range(10)],
+        + [pltpu.SemaphoreType.DMA((n_harm,)) for _ in range(10)]
+        + [pltpu.SemaphoreType.DMA((per_dev, n_harm)) for _ in range(2)],
         compiler_params=pltpu.CompilerParams(
             collective_id=0, has_side_effects=True, vmem_limit_bytes=16 * 2**20
         ),

time: 161 us -> 42.2 us (0.26)
  blocking collectives: 124 us -> 0 us
  Pallas kernels: 19.8 us -> 24.6 us
    all_gather x4 -> x0, blocking collectives: 124 us -> none  [body(): lax.all_gather(array, 'harm', axis=0, tiled=True)]
    pallas_call x1, Pallas kernels: 19.8 us -> 24.6 us  [body(): pl.pallas_call(functools.partial(sky_step, n_harm, n_remap, per_dev), in_...]
where the time goes in v5:
time: 42.2 us; the launch traced here: 42.1 us
  Pallas kernels  24.6 us (58%)
  matrix products  16.6 us (39%)
  local copies, waits for them, and re-layouts  0.85 us (2%)
    pallas_call x1, Pallas kernels, body(): pl.pallas_call(functools.partial(sky_step, n_harm, n_remap, per_dev), in_...  24.6 us
    dot_general x1, matrix products, body(): jnp.einsum('mkl,mrl->rkm', alm, legendre, preferred_element_type=jnp.floa...  16.6 us

profile of v5, /device:TPU:0, one launch (start us, length us, event | category | flops | bytes accessed | tf_op | source)
XLA Modules:
  0.0 42.1 jit_solution(2411115223060108190)
XLA Ops:
  0.0 0.0 copy-start.1
  0.0 0.0 copy-start.2
  0.0 0.0 copy-start
  0.0 0.0 copy-start.6
  0.0 0.0 copy-start.5
  0.0 0.0 copy-start.4
  0.0 0.0 copy-start.3
  0.0 16.6 %fusion = f32[128,8,32]{2,1,0:T(8,128)S(1)} fusion(bf16[128,8,4096]{2,1,0:T(8,128)(2,1)} %param.10, bf16[128,32,4096]{2,1,0:T(8,128)(2,1)} %param.9), kind=kOutput, calls=%fused_computation | convolution fusion | flops 268435456 | bytes 42074112 | tf_op jit(solution)/shard_map/mkl,mrl->rkm/dot_general | solution.py:401
  16.6 0.2 copy.10
  16.8 0.0 copy-done.1
  16.8 0.0 copy-done.2
  16.8 0.0 copy-done
  16.8 0.0 copy-done.6
  16.8 0.0 copy-done.5
  16.8 0.0 copy-done.4
  16.9 0.0 copy-done.3
  16.9 24.6 %shard_map.91 = bf16[16,2048]{1,0:T(8,128)(2,1)S(1)} custom-call(f32[8,32,128]{2,1,0:T(8,128)S(1)} %bitcast.8, s32[16,128]{1,0:T(8,128)S(1)} %bitcast.10, s32[16,128]{1,0:T(8,128)S(1)} %bitcast.11, s32[16,128]{1,0:T(8,128)S(1)} %bitcast.12, s32[16,128]{1,0:T(8,128)S(1)} %bitcast.13, f32[256,384]{1,0:T(8,128)S(1)} %copy-done, f32[2,128,128]{2,1,0:T(8,128)S(1)} %copy-done.2, ...), custom_call_target="tpu_custom_call" | custom-call | tf_op jit(solution)/shard_map/pallas_call | solution.py:403
  41.4 0.6 %copy.12 = bf16[16,1,2048]{2,0,1:T(8,128)(2,1)} copy(bf16[16,1,2048]{2,0,1:T(8,128)(2,1)S(1)} %bitcast.9) | data formatting | bytes 131072
Async XLA Ops:
  0.0 16.8 %copy-start.1 = (f32[4,80,256]{2,1,0:T(8,128)S(1)}, f32[4,80,256]{2,1,0:T(8,128)}, u32[]{:S(2)}) copy-start(f32[4,80,256]{2,1,0:T(8,128)} %constant.8.clone.second_ref) | copy-start | bytes 983044
  0.0 16.8 %copy-start.2 = (f32[2,128,128]{2,1,0:T(8,128)S(1)}, f32[2,128,128]{2,1,0:T(8,128)}, u32[]{:S(2)}) copy-start(f32[2,128,128]{2,1,0:T(8,128)} %constant.7.clone.twist_ref) | copy-start | bytes 393220
  0.0 16.8 %copy-start = (f32[256,384]{1,0:T(8,128)S(1)}, f32[256,384]{1,0:T(8,128)}, u32[]{:S(2)}) copy-start(f32[256,384]{1,0:T(8,128)} %constant.6.clone.first_ref) | copy-start | bytes 1179652
  0.0 16.8 %copy-start.6 = (s32[1,2048]{1,0:T(1,128)S(1)}, s32[1,2048]{1,0:T(1,128)}, u32[]{:S(2)}) copy-start(s32[1,2048]{1,0:T(1,128)} %param.14) | copy-start | bytes 24580
  0.0 16.8 %copy-start.5 = (s32[1,2048]{1,0:T(1,128)S(1)}, s32[1,2048]{1,0:T(1,128)}, u32[]{:S(2)}) copy-start(s32[1,2048]{1,0:T(1,128)} %param.13) | copy-start | bytes 24580
  0.0 16.8 %copy-start.4 = (s32[1,2048]{1,0:T(1,128)S(1)}, s32[1,2048]{1,0:T(1,128)}, u32[]{:S(2)}) copy-start(s32[1,2048]{1,0:T(1,128)} %param.12) | copy-start | bytes 24580
  0.0 16.8 %copy-start.3 = (s32[1,2048]{1,0:T(1,128)S(1)}, s32[1,2048]{1,0:T(1,128)}, u32[]{:S(2)}) copy-start(s32[1,2048]{1,0:T(1,128)} %param.11) | copy-start | bytes 24580

commit v6 on v1

--- a/solution.py
+++ b/solution.py
@@ -321,11 +321,14 @@
             )
         for i, ref in enumerate((sc_ref, sp_ref, oc_ref, op_ref)):
             where_ref[me, i] = ref[...]
-        pl.semaphore_wait(barrier, n_harm + 1)
+
+    accumulate_orders(group, alm_ref, leg_ref, acc_ref)
+
+    @pl.when(group == 0)
+    def _():
+        pl.semaphore_wait(pltpu.get_barrier_semaphore(), n_harm + 1)
         for p in peers:
             index_copy(me, p).start()
-
-    accumulate_orders(group, alm_ref, leg_ref, acc_ref)
 
     @pl.when(group == pl.num_programs(0) - 1)
     def _():
@@ -371,7 +374,7 @@
                 u_ref[e, 1, j] = jnp.where(lane < LANES // 4, w_ref[9 : 9 + tiles, cols], here)
         for r in range(cycles):
             for e in range(per_dev):
-                maps_ref[r, e] = interpolate(
+                maps_ref[r, e * tiles : (e + 1) * tiles, :] = interpolate(
                     e, r, cycles, u_ref,
                     where_ref[r, 0], where_ref[r, 1], where_ref[r, 2], where_ref[r, 3], tiles,
                 )
@@ -383,11 +386,10 @@
         fin_ref[me] = maps_ref[me]
         for p in peers:
             map_copy(p, p).wait_recv()
-        for s in range(sims):
-            for t in range(tiles):
-                out_ref[s : s + 1, t * LANES : (t + 1) * LANES] = fin_ref[
-                    s // per_dev, s % per_dev, t : t + 1
-                ].astype(jnp.bfloat16)
+        for t in range(tiles):
+            out_ref[:, t * LANES : (t + 1) * LANES] = jnp.concatenate(
+                [fin_ref[h, pl.ds(t, per_dev, stride=tiles), :] for h in range(n_harm)], axis=0
+            ).astype(jnp.bfloat16)
         for p in peers:
             index_copy(me, p).wait_send()
             order_copy(me, p).wait_send()
@@ -431,8 +433,8 @@
             pltpu.VMEM((2, cycles * LANES, 2 * LANES), jnp.bfloat16),
             pltpu.VMEM((tiles + 16, cycles * LANES), jnp.float32),
             pltpu.VMEM((per_dev, 2, cycles, tiles, LANES), jnp.float32),
-            pltpu.VMEM((cycles, per_dev, tiles, LANES), jnp.float32),
-            pltpu.VMEM((n_harm, per_dev, tiles, LANES), jnp.float32),
+            pltpu.VMEM((cycles, per_dev * tiles, LANES), jnp.float32),
+            pltpu.VMEM((n_harm, per_dev * tiles, LANES), jnp.float32),
         ]
         + sems,
         compiler_params=pltpu.CompilerParams(

time: 41 us -> 39.5 us (0.963)
  Pallas kernels: 39.4 us -> 37.9 us
    pallas_call x1, Pallas kernels: 39.4 us -> 37.9 us  [body(): pl.pallas_call(functools.partial(sky_step, n_harm, n_remap, per_dev), gri...]
where the time goes in v6:
time: 39.5 us; the launch traced here: 39.4 us
  Pallas kernels  37.9 us (96%)
  local copies, waits for them, and re-layouts  1.47 us (4%)
    pallas_call x1, Pallas kernels, body(): pl.pallas_call(functools.partial(sky_step, n_harm, n_remap, per_dev), gri...  37.9 us
    unnamed x1, local copies, waits for them, and re-layouts  1.47 us

profile of v6, /device:TPU:0, one launch (start us, length us, event | category | flops | bytes accessed | tf_op | source)
XLA Modules:
  0.0 39.4 jit_solution(9684058835514120192)
XLA Ops:
  0.0 37.9 %shard_map.91 = bf16[16,2048]{1,0:T(8,128)(2,1)} custom-call(bf16[16,8,32,4096]{3,2,1,0:T(8,128)(2,1)} %bitcast.7, bf16[16,8,8,4096]{3,2,1,0:T(8,128)(2,1)} %bitcast.8, s32[16,128]{1,0:T(8,128)} %bitcast.10, s32[16,128]{1,0:T(8,128)} %bitcast.11, s32[16,128]{1,0:T(8,128)} %bitcast.12, s32[16,128]{1,0:T(8,128)} %bitcast.13, ...), custom_call_target="tpu_custom_call" | custom-call | tf_op jit(solution)/shard_map/pallas_call | solution.py:418
  37.9 1.5 %copy.11 = bf16[16,1,2048]{2,0,1:T(8,128)(2,1)} copy(bf16[16,1,2048]{2,0,1:T(8,128)(2,1)} %bitcast.9) | data formatting | bytes 131072
